TPU v7x, 32 devices: a whole 2x2x4 slice. The times are simulated.
32 devices in a mesh: grp: 4 (over x, core), inner: 8 (over z, y).
Axes of the slice: x: 2, y: 2, z: 4, core: 2. Of those that a mesh axis runs over, the one named last changes fastest.
Arguments:
- electric: float32 [3, 16, 128, 512], P(None, None, 'inner', 'grp'), may hold values from -6 to 6
- magnetic: float32 [3, 16, 128, 512], P(None, None, 'inner', 'grp'), may hold values from -6 to 6
- material_ids: int32 [16, 128, 512], P(None, 'inner', 'grp'), may hold values from 0 to 7
- update_ca: float32 [8], replicated, may hold values from 0.6 to 1
- update_cb: float32 [8], replicated, may hold values from 0.12 to 0.45
- face_ranges: int32 [8, 4, 4], P('inner', 'grp'), may hold values from 0 to 128, as said below
- band_table: int32 [32], replicated, may hold values from 0 to 31, each once
Outputs:
- electric_out: float32 [3, 16, 128, 512], P(None, None, 'inner', 'grp')
- magnetic_out: float32 [3, 16, 128, 512], P(None, None, 'inner', 'grp')
- far_field: float32 [32, 8, 128], P(('grp', 'inner'))
Inputs may be any that keep to these rules, and one draw needn't show every extreme that they name: `face_ranges`: one box [x0, x1) x [y0, y1) with x0 <= 32, x1 >= 96, y0 <= 128, y1 >= 384 is clipped to each tile: entries are (clip(x0 - i * 16), clip(x1 - i * 16), clip(y0 - j * 128), clip(y1 - j * 128)), each clip into [0, tile width].
All inputs are finite; a program needn't handle non-finite values.
Results may differ from a plain program's by a relative error of at most 0.0003.
Values sent between devices are 32-bit elements; how exact they have to be, the bound alone decides.
A program may use at most 64 MiB of HBM per device.

v0:
```python
import functools
import math

import jax
import jax.numpy as jnp
import numpy as np
from jax import lax
from jax.experimental import pallas as pl
from jax.experimental.pallas import tpu as pltpu
from jax.sharding import PartitionSpec as P

STEPS = 8
FREQS = 32
ANG_BAND = 4
NMAT = 8
ZF = 8
NZ = 16
CX = 16
CY = 128
PITCH = 24
BASE = 8
MESH = pl.DeviceIdType.MESH


def tables(bands, groups):
    f = np.tile(np.arange(FREQS, dtype=np.int64) + 1, ANG_BAND)
    b = np.repeat(np.arange(ANG_BAND, dtype=np.int64) * 33 // ANG_BAND - 16, FREQS)
    a = np.arange(bands, dtype=np.int64) - bands // 2

    def both(turns, period):
        angle = (turns % period) * (2.0 * math.pi / period)
        return np.cos(angle).astype(np.float32), np.sin(angle).astype(np.float32)

    y = np.arange(CY, dtype=np.int64)[:, None]
    proj = np.concatenate(both(f * b * y, 4096), axis=1)
    time = np.stack(both(f * np.arange(STEPS, dtype=np.int64)[:, None], 128))
    y_start = np.stack(both(f * b * CY * np.arange(groups, dtype=np.int64)[:, None], 4096))
    cell = np.stack(both(f * a[:, None], 4096))
    block = np.stack(both(f * a[:, None] * CX, 4096))
    flat = [proj[:, :CY], proj[:, CY:]] + [part for table in (time, y_start, cell, block) for part in table]
    starts = np.cumsum([0] + [-(-part.shape[0] // 8) * 8 for part in flat])
    packed = np.zeros((starts[-1], CY), np.float32)
    for start, part in zip(starts, flat):
        packed[start : start + part.shape[0]] = part
    return packed, tuple(int(start) for start in starts[:-1])


class Rows:
    def __init__(self, ref, starts):
        self.ref, self.starts = ref, starts

    def at(self, part, first, count):
        return self.ref[pl.ds(self.starts[part] + first, count), :]


def kernel(
    ny, nx, scale, starts,
    e_hbm, h_hbm, ids_hbm, ca_hbm, cb_hbm, face_hbm, bands_hbm, table_hbm,
    e_out, h_out, far_out,
    e_in, h_in, ids, ca, cb, face, bands, table, in_sem,
    ep, hp, coef_a, coef_b,
    xs_r, xs_l, ys_r, ys_l, xr_l, xr_r, yr_l, yr_r, cor_x, cor_y,
    sample, acc, cols, phase, f_send, f_recv,
    send_sem, recv_sem, f_send_sem, f_recv_sem, hx_send, hx_recv, once_sem,
):
    iy = lax.axis_index("grp")
    ix = lax.axis_index("inner")
    total = ny * nx
    me = iy * nx + ix
    lane = lax.broadcasted_iota(jnp.int32, (CX, CY), 1)
    row = lax.broadcasted_iota(jnp.int32, (CX, CY), 0)

    loads = [
        pltpu.make_async_copy(src, dst, in_sem.at[i])
        for i, (src, dst) in enumerate(
            (
                (e_hbm, e_in),
                (h_hbm, h_in),
                (ids_hbm, ids),
                (ca_hbm, ca),
                (cb_hbm, cb),
                (face_hbm, face),
                (bands_hbm, bands),
                (table_hbm, table),
            )
        )
    ]
    for load in loads:
        load.start()
    time, y_start, cell, block = (Rows(table, starts[i : i + 2]) for i in (2, 4, 6, 8))

    for buf in (hx_recv, xr_l, xr_r, yr_l, yr_r, cor_x, cor_y):
        buf[...] = jnp.zeros(buf.shape, jnp.float32)

    barrier = pltpu.get_barrier_semaphore()

    def greet(k, carry):
        other = lax.rem(me + k, total)
        pl.semaphore_signal(
            barrier, inc=1, device_id=(lax.div(other, nx), lax.rem(other, nx)), device_id_type=MESH
        )
        return carry

    lax.fori_loop(1, total, greet, 0)

    def at(z, shift=0):
        return pl.ds(z * PITCH + BASE + shift, CX)

    def plane(x):
        return pl.ds(BASE + x, NZ, stride=PITCH)

    for c in (1, 2):
        ep[c, plane(CX), :] = jnp.zeros((NZ, CY), jnp.float32)
    for load in loads:
        load.wait()
    for c in range(3):
        for z in range(NZ):
            ep[c, at(z), :] = e_in[c, pl.ds(z * CX, CX), :]
            hp[c, at(z), :] = h_in[c, pl.ds(z * CX, CX), :]
    for z in range(NZ):
        here = ids[pl.ds(z * CX, CX), :]
        va = jnp.zeros((CX, CY), jnp.float32)
        vb = jnp.zeros((CX, CY), jnp.float32)
        for m in range(NMAT):
            chosen = here == m
            va = jnp.where(chosen, ca[m], va)
            vb = jnp.where(chosen, cb[m], vb)
        coef_a[pl.ds(z * CX, CX), :] = va
        coef_b[pl.ds(z * CX, CX), :] = vb
    sample[...] = jnp.zeros(sample.shape, jnp.float32)
    acc[...] = jnp.zeros(acc.shape, jnp.float32)
    on_face = (row >= face[0]) & (row < face[1]) & (lane >= face[2]) & (lane < face[3])
    inside_x = jnp.where(ix > 0, 1.0, 0.0).astype(jnp.float32)
    inside_y = jnp.where(iy > 0, 1.0, 0.0).astype(jnp.float32)

    def power(bit, carry):
        pr, pi, br, bi = carry
        take = lax.rem(lax.shift_right_logical(ix, bit), 2) == 1
        nr = pr * br - pi * bi
        ni = pr * bi + pi * br
        return (
            jnp.where(take, nr, pr),
            jnp.where(take, ni, pi),
            br * br - bi * bi,
            2.0 * br * bi,
        )

    rows_at_once = 8
    for start in range(0, total, rows_at_once):
        part = pl.ds(start, rows_at_once)
        carry = (
            jnp.full((rows_at_once, CY), scale, jnp.float32),
            jnp.zeros((rows_at_once, CY), jnp.float32),
            block.at(0, start, rows_at_once),
            block.at(1, start, rows_at_once),
        )
        for bit in range(max(1, (nx - 1).bit_length())):
            carry = power(bit, carry)
        phase[part, :] = carry[0]
        phase[pl.ds(total + start, rows_at_once), :] = carry[1]

    start_phase = Rows(phase, (0, total))
    pl.semaphore_wait(barrier, total - 1)

    has_xr, has_xl = ix < nx - 1, ix > 0
    has_yr, has_yl = iy < ny - 1, iy > 0

    def copies(n):
        return (
            (has_xr, has_xl, xs_r.at[n], xr_l.at[n], (iy, ix + 1)),
            (has_xl, has_xr, xs_l.at[n], xr_r.at[n], (iy, ix - 1)),
            (has_yr, has_yl, ys_r.at[n], yr_l.at[n], (iy + 1, ix)),
            (has_yl, has_yr, ys_l.at[n], yr_r.at[n], (iy - 1, ix)),
            (has_xr & has_yl, has_xl & has_yr, xs_r.at[n, pl.ds(0, NZ)], cor_x.at[n], (iy - 1, ix + 1)),
            (has_xl & has_yr, has_xr & has_yl, ys_r.at[n, pl.ds(0, 8)], cor_y.at[n], (iy + 1, ix - 1)),
        )

    def remote(n, i, src, dst, device):
        return pltpu.make_async_remote_copy(
            src_ref=src,
            dst_ref=dst,
            send_sem=send_sem.at[i],
            recv_sem=recv_sem.at[n, i],
            device_id=device,
            device_id_type=MESH,
        )

    def start_copies(n, which):
        every = copies(n)
        for i in which:
            sends, _, src, dst, device = every[i]

            @pl.when(sends)
            def _(i=i, src=src, dst=dst, device=device):
                remote(n, i, src, dst, device).start()

    def add_sample(n):
        g_re, g_im = (
            jnp.dot(
                sample[...],
                table[pl.ds(starts[part], CY), :],
                precision=lax.Precision.HIGHEST,
                preferred_element_type=jnp.float32,
            )
            for part in range(2)
        )
        ct, st = time.at(0, n, 1), time.at(1, n, 1)
        acc[0] += ct * g_re + st * g_im
        acc[1] += ct * g_im - st * g_re

    def step(n, carry):
        last = jnp.zeros((CX, CY), jnp.float32)
        first = jnp.zeros((CX, CY), jnp.float32)
        for c in range(3):
            xs_r[n, pl.ds(c * NZ, NZ), :] = ep[c, plane(CX - 1), :]
        for g, c in enumerate((1, 2)):
            xs_l[n, pl.ds(g * NZ, NZ), :] = ep[c, plane(0), :]
        start_copies(n, (4, 0, 1))
        for z in range(NZ):
            for g, (field, c) in enumerate(((ep, 0), (ep, 1), (ep, 2), (hp, 0), (hp, 2))):
                spot = g * NZ + z
                last = jnp.where(lane == spot, pltpu.roll(field[c, at(z), :], (spot - CY + 1) % CY, 1), last)
            for g, c in enumerate((0, 2)):
                spot = g * NZ + z
                value = ep[c, at(z), :]
                first = jnp.where(lane == spot, pltpu.roll(value, spot, 1) if spot else value, first)
        ys_r[n] = last
        ys_l[n] = first
        start_copies(n, (5, 2, 3))

        zero = jnp.zeros((CX, CY), jnp.float32)
        for z in range(NZ):
            ex, ey, ez = (ep[c, at(z), :] for c in range(3))
            ex_z = ep[0, at(z + 1), :] if z < NZ - 1 else zero
            ey_z = ep[1, at(z + 1), :] if z < NZ - 1 else zero
            ey_x = ep[1, at(z, 1), :]
            ez_x = ep[2, at(z, 1), :]
            ex_y = jnp.where(lane == CY - 1, 0.0, pltpu.roll(ex, CY - 1, 1))
            ez_y = jnp.where(lane == CY - 1, 0.0, pltpu.roll(ez, CY - 1, 1))
            hp[0, at(z), :] = hp[0, at(z), :] - 0.5 * ((ez_y - ez) - (ey_z - ey))
            hp[1, at(z), :] = hp[1, at(z), :] - 0.5 * ((ex_z - ex) - (ez_x - ez))
            hp[2, at(z), :] = hp[2, at(z), :] - 0.5 * ((ey_x - ey) - (ex_y - ex))
        add_sample(jnp.maximum(n - 1, 0))

        for i, (_, receives, src, dst, _) in enumerate(copies(n)):
            @pl.when(receives)
            def _(i=i, src=src, dst=dst):
                remote(n, i, src, dst, (iy, ix)).wait_recv()

        @pl.when(n == 0)
        def _():
            @pl.when(has_xl)
            def _():
                once.wait_recv()

            for g, c in enumerate((1, 2)):
                hp[c, plane(-1), :] = hx_recv[pl.ds(g * NZ, NZ), :]

        ex, ey, ez = (xr_l[n, pl.ds(g * NZ, NZ), :] for g in range(3))
        hy, hz = hp[1, plane(-1), :], hp[2, plane(-1), :]
        ey0, ez0 = xs_l[n, pl.ds(0, NZ), :], xs_l[n, pl.ds(NZ, NZ), :]
        hp[1, plane(CX - 1), :] += 0.5 * xr_r[n, pl.ds(NZ, NZ), :]
        hp[2, plane(CX - 1), :] -= 0.5 * xr_r[n, pl.ds(0, NZ), :]
        ex_z = jnp.where(row == NZ - 1, 0.0, pltpu.roll(ex, NZ - 1, 0))
        ex_y = pltpu.roll(jnp.where(lane == 0, cor_x[n], ex), CY - 1, 1)
        hp[1, plane(-1), :] = inside_x * (hy - 0.5 * ((ex_z - ex) - (ez0 - ez)))
        hp[2, plane(-1), :] = inside_x * (hz - 0.5 * ((ey0 - ey) - (ex_y - ex)))

        packed, own = yr_l[n], ys_l[n]
        ex = packed
        ey, ez, hx, hz = (pltpu.roll(packed, CY - g * NZ, 1) for g in range(1, 5))
        ex0, ez0 = own, pltpu.roll(own, CY - NZ, 1)
        ey_z = jnp.where(lane == NZ - 1, 0.0, pltpu.roll(ey, CY - 1, 1))
        corner = pltpu.roll(cor_y[n], CY - NZ, 1)[0:1, :]
        ey_x = jnp.where(row == CX - 1, corner, pltpu.roll(ey, CX - 1, 0))
        hx_col = inside_y * (hx - 0.5 * ((ez0 - ez) - (ey_z - ey)))
        hz_col = inside_y * (hz - 0.5 * ((ey_x - ey) - (ex0 - ex)))

        after = 0.5 * yr_r[n]
        for z in range(NZ):
            hy = hp[1, at(z), :]
            hx = hp[0, at(z), :] - jnp.where(lane == CY - 1, pltpu.roll(after, CY - 1 - NZ - z, 1), 0.0)
            hz = hp[2, at(z), :] + jnp.where(lane == CY - 1, pltpu.roll(after, CY - 1 - z, 1), 0.0)
            hp[0, at(z), :] = hx
            hp[2, at(z), :] = hz
            hx_z = hp[0, at(z - 1), :] if z else zero
            hy_z = hp[1, at(z - 1), :] if z else zero
            hy_x = hp[1, at(z, -1), :]
            hz_x = hp[2, at(z, -1), :]
            hx_y = jnp.where(lane == 0, pltpu.roll(hx_col, CY - z, 1) if z else hx_col, pltpu.roll(hx, 1, 1))
            hz_y = jnp.where(lane == 0, pltpu.roll(hz_col, CY - z, 1) if z else hz_col, pltpu.roll(hz, 1, 1))
            va, vb = coef_a[pl.ds(z * CX, CX), :], coef_b[pl.ds(z * CX, CX), :]
            ex = va * ep[0, at(z), :] + vb * ((hz - hz_y) - (hy - hy_z))
            ey = va * ep[1, at(z), :] + vb * ((hx - hx_z) - (hz - hz_x))
            ep[0, at(z), :] = ex
            ep[1, at(z), :] = ey
            ep[2, at(z), :] = va * ep[2, at(z), :] + vb * ((hy - hy_x) - (hx - hx_y))
            if z == ZF:
                for c, value in enumerate((ex, ey, hx, hy)):
                    sample[pl.ds(c * CX, CX), :] = jnp.where(on_face, value, 0.0)

        for i, (sends, _, src, dst, device) in enumerate(copies(n)):
            @pl.when(sends)
            def _(i=i, src=src, dst=dst, device=device):
                remote(n, i, src, dst, device).wait_send()
        return carry

    once = pltpu.make_async_remote_copy(
        src_ref=hx_send,
        dst_ref=hx_recv,
        send_sem=once_sem.at[0],
        recv_sem=once_sem.at[1],
        device_id=(iy, ix + 1),
        device_id_type=MESH,
    )
    for g, c in enumerate((1, 2)):
        hx_send[pl.ds(g * NZ, NZ), :] = hp[c, plane(CX - 1), :]

    @pl.when(has_xr)
    def _():
        once.start()

    lax.fori_loop(0, STEPS, step, 0)

    @pl.when(has_xr)
    def _():
        once.wait_send()

    add_sample(STEPS - 1)

    yr, yi = y_start.at(0, iy, 1), y_start.at(1, iy, 1)
    col_re = acc[0] * yr - acc[1] * yi
    acc[1] = acc[0] * yi + acc[1] * yr
    acc[0] = col_re
    for part in range(2):
        for x in range(CX):
            four = acc[part, pl.ds(x, 4, stride=CX), :]
            cols[part, x, pl.ds(0, 4), :] = four
            cols[part, x, pl.ds(4, 4), :] = four

    upper = lax.broadcasted_iota(jnp.int32, (8, CY), 0) < 4
    at_once = min(8, total)

    def send_far(k):
        other = lax.rem(me + k, total)
        return pltpu.make_async_remote_copy(
            src_ref=f_send.at[k],
            dst_ref=f_recv.at[k - 1],
            send_sem=f_send_sem,
            recv_sem=f_recv_sem,
            device_id=(lax.div(other, nx), lax.rem(other, nx)),
            device_id_type=MESH,
        )

    def project(trip, carry):
        k0 = trip * at_once
        picked = [bands[lax.rem(me + k0 + j, total)] for j in range(at_once)]

        def pair(rows, part, j):
            return jnp.where(upper, rows.at(part, picked[j], 1), rows.at(part, picked[j + 1], 1))

        pairs = range(0, at_once, 2)
        wr = [pair(cell, 0, j) for j in pairs]
        wi = [pair(cell, 1, j) for j in pairs]
        c_re, c_im = cols[0, CX - 1], cols[1, CX - 1]
        re = [c_re for _ in pairs]
        im = [c_im for _ in pairs]
        for x in range(CX - 2, -1, -1):
            c_re, c_im = cols[0, x], cols[1, x]
            re, im = (
                [r * a - i * b + c_re for r, i, a, b in zip(re, im, wr, wi)],
                [r * b + i * a + c_im for r, i, a, b in zip(re, im, wr, wi)],
            )
        for t, j in enumerate(pairs):
            pr, pi = pair(start_phase, 0, j), pair(start_phase, 1, j)
            far_re = re[t] * pr - im[t] * pi
            far_im = re[t] * pi + im[t] * pr
            f_send[k0 + j] = jnp.where(upper, far_re, pltpu.roll(far_im, 4, 0))
            f_send[k0 + j + 1] = jnp.where(upper, pltpu.roll(far_re, 4, 0), far_im)
        for j in range(at_once):
            @pl.when(k0 + j > 0)
            def _(j=j):
                send_far(k0 + j).start()
        return carry

    lax.fori_loop(0, total // at_once, project, 0)

    for c in range(3):
        for z in range(NZ):
            e_out[c, pl.ds(z * CX, CX), :] = ep[c, at(z), :]
            h_out[c, pl.ds(z * CX, CX), :] = hp[c, at(z), :]

    pltpu.make_async_copy(f_recv, f_recv, f_recv_sem).wait()
    if total <= 64:
        terms = [f_send[0]] + [f_recv[k] for k in range(total - 1)]
        while len(terms) > 1:
            terms = [a + b for a, b in zip(terms[::2], terms[1::2])]
        far_out[...] = terms[0]
    else:
        far_out[...] = lax.fori_loop(0, total - 1, lambda k, t: t + f_recv[k], f_send[0])
    pltpu.make_async_copy(f_recv, f_recv, f_send_sem).wait()


def local(ny, nx, electric, magnetic, material_ids, update_ca, update_cb, face_ranges, band_table):
    total = ny * nx
    bands = band_table.shape[0]
    assert bands == total and electric.shape == (3, NZ, CX, CY)
    scale = 1.0 / math.sqrt(CX * nx * CY * ny)
    f32 = jnp.float32
    vmem = pl.BlockSpec(memory_space=pltpu.VMEM)
    hbm = pl.BlockSpec(memory_space=pltpu.HBM)
    packed, starts = tables(bands, ny)
    rows = NZ * CX
    e_out, h_out, far = pl.pallas_call(
        functools.partial(kernel, ny, nx, scale, starts),
        out_shape=(
            jax.ShapeDtypeStruct((3, rows, CY), f32),
            jax.ShapeDtypeStruct((3, rows, CY), f32),
            jax.ShapeDtypeStruct((8, CY), f32),
        ),
        in_specs=[hbm] * 8,
        out_specs=(vmem, vmem, vmem),
        scratch_shapes=[
            pltpu.VMEM((3, rows, CY), f32),
            pltpu.VMEM((3, rows, CY), f32),
            pltpu.VMEM((rows, CY), jnp.int32),
            pltpu.SMEM((NMAT,), f32),
            pltpu.SMEM((NMAT,), f32),
            pltpu.SMEM((4,), jnp.int32),
            pltpu.SMEM((bands,), jnp.int32),
            pltpu.VMEM(packed.shape, f32),
            pltpu.SemaphoreType.DMA((8,)),
            pltpu.VMEM((3, NZ * PITCH + 8, CY), f32),
            pltpu.VMEM((3, NZ * PITCH + 8, CY), f32),
            pltpu.VMEM((rows, CY), f32),
            pltpu.VMEM((rows, CY), f32),
            pltpu.VMEM((STEPS, 3 * NZ, CY), f32),
            pltpu.VMEM((STEPS, 2 * NZ, CY), f32),
            pltpu.VMEM((STEPS, CX, CY), f32),
            pltpu.VMEM((STEPS, CX, CY), f32),
            pltpu.VMEM((STEPS, 3 * NZ, CY), f32),
            pltpu.VMEM((STEPS, 2 * NZ, CY), f32),
            pltpu.VMEM((STEPS, CX, CY), f32),
            pltpu.VMEM((STEPS, CX, CY), f32),
            pltpu.VMEM((STEPS, NZ, CY), f32),
            pltpu.VMEM((STEPS, 8, CY), f32),
            pltpu.VMEM((4 * CX, CY), f32),
            pltpu.VMEM((2, 4 * CX, CY), f32),
            pltpu.VMEM((2, CX, 8, CY), f32),
            pltpu.VMEM((2 * total, CY), f32),
            pltpu.VMEM((total, 8, CY), f32),
            pltpu.VMEM((total - 1, 8, CY), f32),
            pltpu.SemaphoreType.DMA((6,)),
            pltpu.SemaphoreType.DMA((STEPS, 6)),
            pltpu.SemaphoreType.DMA,
            pltpu.SemaphoreType.DMA,
            pltpu.VMEM((2 * NZ, CY), f32),
            pltpu.VMEM((2 * NZ, CY), f32),
            pltpu.SemaphoreType.DMA((2,)),
        ],
        compiler_params=pltpu.CompilerParams(
            collective_id=0, has_side_effects=True, vmem_limit_bytes=62 * 1024 * 1024
        ),
        name="fdtd",
    )(
        electric.reshape(3, rows, CY),
        magnetic.reshape(3, rows, CY),
        material_ids.reshape(rows, CY),
        update_ca,
        update_cb,
        face_ranges.reshape(4),
        band_table,
        packed,
    )
    return (
        e_out.reshape(electric.shape),
        h_out.reshape(electric.shape),
        far.reshape(1, 8, CY),
    )


def solution(mesh):
    in_specs = (
        P(None, None, "inner", "grp"),
        P(None, None, "inner", "grp"),
        P(None, "inner", "grp"),
        P(),
        P(),
        P("inner", "grp", None),
        P(),
    )
    out_specs = (
        P(None, None, "inner", "grp"),
        P(None, None, "inner", "grp"),
        P(("grp", "inner"), None, None),
    )
    body = functools.partial(local, mesh.shape["grp"], mesh.shape["inner"])
    return jax.shard_map(body, mesh=mesh, in_specs=in_specs, out_specs=out_specs, check_vma=False)
```

profile of v0, /device:TPU:0, one launch (start us, length us, event | category | flops | bytes accessed | tf_op | source)
XLA Modules:
  0.0 49.6 jit_solution(5922673902874965263)
XLA Ops:
  0.6 45.8 %fdtd.1 = (f32[3,256,128]{2,1,0:T(8,128)}, f32[3,256,128]{2,1,0:T(8,128)}, f32[8,128]{1,0:T(8,128)}) custom-call(f32[3,256,128]{2,1,0:T(8,128)} %bitcast.7, f32[3,256,128]{2,1,0:T(8,128)} %bitcast.8, s32[256,128]{1,0:T(8,128)} %bitcast.11, f32[8]{0:T(128)} %ca_hbm.1, f32[8]{0:T(128)} %cb_hbm.1, s32[4]{0:T(128)} %bitcast.13, s32[32]{0:T(128)} %bands_hbm.1, ...), custom_call_target="tpu_custom_call" | custom-call | tf_op jit(solution)/shard_map/fdtd/pallas_call | solution.py:414
  46.4 0.0 copy-start
  46.4 1.8 %copy.14 = f32[3,16,16,128]{3,2,1,0:T(8,128)} copy(f32[3,16,16,128]{3,2,1,0:T(8,128)} %bitcast.10) | data formatting | bytes 786432
  48.2 0.0 copy-done
  48.2 0.0 copy-start.1
  48.2 0.7 %copy.15 = f32[3,16,16,128]{3,2,1,0:T(8,128)} copy(f32[3,16,16,128]{3,2,1,0:T(8,128)S(1)} %bitcast.9) | data formatting | bytes 786432
  49.0 0.0 copy-done.1
  49.0 0.6 %copy.16 = f32[1,8,128]{2,1,0:T(8,128)} copy(f32[1,8,128]{2,1,0:T(8,128)S(1)} %bitcast.12) | data formatting | bytes 8192
Async XLA Ops:
  46.4 1.8 %copy-start = (f32[3,256,128]{2,1,0:T(8,128)S(1)}, f32[3,256,128]{2,1,0:T(8,128)}, u32[]{:S(2)}) copy-start(f32[3,256,128]{2,1,0:T(8,128)} %get-tuple-element.7) | copy-start | bytes 1179652
  48.2 0.8 %copy-start.1 = (f32[8,128]{1,0:T(8,128)S(1)}, f32[8,128]{1,0:T(8,128)}, u32[]{:S(2)}) copy-start(f32[8,128]{1,0:T(8,128)} %get-tuple-element.8) | copy-start | bytes 12292
where the time goes:
time: 49.7 us; the launch traced here: 49.6 us
  Pallas kernels  45.8 us (92%)
  local copies, waits for them, and re-layouts  3.16 us (6%)
  between operations  0.65 us (1%)
    pallas_call x1, Pallas kernels, local(): pl.pallas_call(functools.partial(kernel, ny, nx, scale, starts), out_shap...  45.8 us
    unnamed x7, local copies, waits for them, and re-layouts  3.16 us

commit v1 on v0

v1 whole, which is shorter than its diff:
```python
import functools
import math

import jax
import jax.numpy as jnp
import numpy as np
from jax import lax
from jax.experimental import pallas as pl
from jax.experimental.pallas import tpu as pltpu
from jax.sharding import PartitionSpec as P

STEPS = 8
FREQS = 32
ANG_BAND = 4
NMAT = 8
ZF = 8
NZ = 16
CX = 16
CY = 128
PAD = 8
HALO = 8
ROWS = CX + 2 * HALO
PITCH = ROWS + 2 * PAD
GROUPS = ROWS // 8
OWN = (1, 2)
HALF = NZ // 2
SIDE = CY // 4
MESH = pl.DeviceIdType.MESH


def tables(bands, groups):
    f = np.tile(np.arange(FREQS, dtype=np.int64) + 1, ANG_BAND)
    b = np.repeat(np.arange(ANG_BAND, dtype=np.int64) * 33 // ANG_BAND - 16, FREQS)
    a = np.arange(bands, dtype=np.int64) - bands // 2

    def both(turns, period):
        angle = (turns % period) * (2.0 * math.pi / period)
        return np.cos(angle).astype(np.float32), np.sin(angle).astype(np.float32)

    y = np.arange(CY, dtype=np.int64)[:, None]
    proj = np.concatenate(both(f * b * y, 4096), axis=1)
    time = np.stack(both(f * np.arange(STEPS, dtype=np.int64)[:, None], 128))
    y_start = np.stack(both(f * b * CY * np.arange(groups, dtype=np.int64)[:, None], 4096))
    cell = np.stack(both(f * a[:, None], 4096))
    block = np.stack(both(f * a[:, None] * CX, 4096))
    flat = [proj[:, :CY], proj[:, CY:]] + [part for table in (time, y_start, cell, block) for part in table]
    starts = np.cumsum([0] + [-(-part.shape[0] // 8) * 8 for part in flat])
    packed = np.zeros((starts[-1], CY), np.float32)
    for start, part in zip(starts, flat):
        packed[start : start + part.shape[0]] = part
    return packed, tuple(int(start) for start in starts[:-1])


class Rows:
    def __init__(self, ref, starts):
        self.ref, self.starts = ref, starts

    def at(self, part, first, count):
        return self.ref[pl.ds(self.starts[part] + first, count), :]


def kernel(
    ny, nx, scale, starts,
    e_hbm, h_hbm, ids_hbm, ca_hbm, cb_hbm, face_hbm, bands_hbm, table_hbm,
    e_out, h_out, far_out,
    ef, hf, ids, ca, cb, face, bands, table, in_sem,
    coef_a, coef_b, se, sh, strip_a, strip_b,
    edge_r, edge_l, from_l, from_r,
    sample, acc, cols, phase, f_send, f_recv,
    send_sem, recv_sem, f_send_sem, f_recv_sem, out_sem,
):
    iy = lax.axis_index("grp")
    ix = lax.axis_index("inner")
    total = ny * nx
    me = iy * nx + ix
    f32 = jnp.float32
    lane = lax.broadcasted_iota(jnp.int32, (8, CY), 1)
    row = lax.broadcasted_iota(jnp.int32, (8, CY), 0)
    own_rows = pl.ds(PAD + HALO, CX)

    loads = [
        pltpu.make_async_copy(src, dst, in_sem.at[i])
        for i, (src, dst) in enumerate(
            (
                (e_hbm, ef.at[:, :, own_rows]),
                (h_hbm, hf.at[:, :, own_rows]),
                (ids_hbm, ids.at[:, pl.ds(HALO, CX)]),
                (ca_hbm, ca),
                (cb_hbm, cb),
                (face_hbm, face),
                (bands_hbm, bands),
                (table_hbm, table),
            )
        )
    ]
    for load in loads:
        load.start()
    time, y_start, cell, block = (Rows(table, starts[i : i + 2]) for i in (2, 4, 6, 8))

    barrier = pltpu.get_barrier_semaphore()

    def greet(k, carry):
        other = lax.rem(me + k, total)
        pl.semaphore_signal(
            barrier, inc=1, device_id=(lax.div(other, nx), lax.rem(other, nx)), device_id_type=MESH
        )
        return carry

    lax.fori_loop(1, total, greet, 0)

    has_xr, has_xl = ix < nx - 1, ix > 0
    has_yr, has_yl = iy < ny - 1, iy > 0
    low, high = pl.ds(0, 8), pl.ds(8, 8)
    every = (
        (has_yr, has_yl, edge_r, from_l.at[:, pl.ds(HALO, CX)], (iy + 1, ix)),
        (has_yr & has_xr, has_yl & has_xl, edge_r.at[:, high], from_l.at[:, low], (iy + 1, ix + 1)),
        (has_yr & has_xl, has_yl & has_xr, edge_r.at[:, low], from_l.at[:, pl.ds(24, 8)], (iy + 1, ix - 1)),
        (has_yl, has_yr, edge_l, from_r.at[:, pl.ds(HALO, CX)], (iy - 1, ix)),
        (has_yl & has_xr, has_yr & has_xl, edge_l.at[:, high], from_r.at[:, low], (iy - 1, ix + 1)),
        (has_yl & has_xl, has_yr & has_xr, edge_l.at[:, low], from_r.at[:, pl.ds(24, 8)], (iy - 1, ix - 1)),
        (has_xr, has_xl, e_hbm.at[:, :, high], ef.at[:, :, pl.ds(PAD, 8)], (iy, ix + 1)),
        (has_xl, has_xr, e_hbm.at[:, :, low], ef.at[:, :, pl.ds(PAD + 24, 8)], (iy, ix - 1)),
        (has_xr, has_xl, h_hbm.at[:, :, high], hf.at[:, :, pl.ds(PAD, 8)], (iy, ix + 1)),
        (has_xl, has_xr, h_hbm.at[:, :, low], hf.at[:, :, pl.ds(PAD + 24, 8)], (iy, ix - 1)),
        (has_xr, has_xl, ids_hbm.at[:, high], ids.at[:, low], (iy, ix + 1)),
        (has_xl, has_xr, ids_hbm.at[:, low], ids.at[:, pl.ds(24, 8)], (iy, ix - 1)),
    )

    def remote(i, src, dst, device):
        return pltpu.make_async_remote_copy(
            src_ref=src,
            dst_ref=dst,
            send_sem=send_sem.at[i],
            recv_sem=recv_sem.at[i],
            device_id=device,
            device_id_type=MESH,
        )

    def start_copies(which):
        for i in which:
            sends, _, src, dst, device = every[i]

            @pl.when(sends)
            def _(i=i, src=src, dst=dst, device=device):
                remote(i, src, dst, device).start()

    def await_copies(which):
        for i in which:
            _, receives, src, dst, _ = every[i]

            @pl.when(receives)
            def _(i=i, src=src, dst=dst):
                remote(i, src, dst, (iy, ix)).wait_recv()

    y_copies, x_copies = range(6), range(6, 12)

    for missing, rows in (
        (jnp.logical_not(has_xl), 0),
        (jnp.logical_not(has_xr), 24),
    ):
        @pl.when(missing)
        def _(rows=rows):
            def fill(z, carry):
                for c in range(3):
                    ef[c, z, pl.ds(PAD + rows, 8), :] = jnp.zeros((8, CY), f32)
                    hf[c, z, pl.ds(PAD + rows, 8), :] = jnp.zeros((8, CY), f32)
                ids[z, pl.ds(rows, 8), :] = jnp.full((8, CY), NMAT, jnp.int32)
                return carry

            lax.fori_loop(0, NZ, fill, 0)

    for edge, side in ((from_l, has_yl), (from_r, has_yr)):
        for given, rows, count in ((side, 8, 16), (side & has_xl, 0, 8), (side & has_xr, 24, 8)):
            @pl.when(jnp.logical_not(given))
            def _(edge=edge, rows=rows, count=count):
                edge[pl.ds(0, 6), pl.ds(rows, count), :] = jnp.zeros((6, count, CY), f32)
                edge[6, pl.ds(rows, count), :] = jnp.full((count, CY), float(NMAT), f32)

    def clear(z, carry):
        for c in range(3):
            for rows in (0, PAD + ROWS):
                ef[c, z, pl.ds(rows, PAD), :] = jnp.zeros((PAD, CY), f32)
                hf[c, z, pl.ds(rows, PAD), :] = jnp.zeros((PAD, CY), f32)
        return carry

    lax.fori_loop(0, NZ, clear, 0)
    for field in (se, sh):
        for c in range(3):
            for j in range(HALF):
                for rows in (0, PAD + ROWS):
                    field[c, j, pl.ds(rows, PAD), :] = jnp.zeros((PAD, CY), f32)
    sample[...] = jnp.zeros(sample.shape, f32)
    acc[...] = jnp.zeros(acc.shape, f32)

    pl.semaphore_wait(barrier, total - 1)
    start_copies(x_copies)
    for load in loads:
        load.wait()

    for i in range(7):
        for g in range(2):
            right = jnp.zeros((8, CY), f32)
            left = jnp.zeros((8, CY), f32)
            for z in range(NZ):
                rows = pl.ds(8 * g + PAD + HALO, 8)
                if i < 6:
                    value = (ef, hf)[i // 3][i % 3, z, rows, :]
                else:
                    value = ids[z, pl.ds(8 * g + HALO, 8), :].astype(f32)
                here = (lane >= 8 * z) & (lane < 8 * z + 8)
                right = jnp.where(here, pltpu.roll(value, (8 * z - 120) % CY, 1) if z < 15 else value, right)
                left = jnp.where(here, pltpu.roll(value, 8 * z, 1) if z else value, left)
            edge_r[i, pl.ds(8 * g, 8), :] = right
            edge_l[i, pl.ds(8 * g, 8), :] = left
    start_copies(y_copies)

    def lookup(here):
        va = jnp.zeros((8, CY), f32)
        vb = jnp.zeros((8, CY), f32)
        for m in range(NMAT):
            chosen = here == m
            va = jnp.where(chosen, ca[m], va)
            vb = jnp.where(chosen, cb[m], vb)
        return va, vb

    def coefficients(groups):
        def one(z, carry):
            for g in groups:
                va, vb = lookup(ids[z, pl.ds(8 * g, 8), :])
                coef_a[z, pl.ds(8 * g, 8), :] = va
                coef_b[z, pl.ds(8 * g, 8), :] = vb
            return carry

        lax.fori_loop(0, NZ, one, 0)

    in_half = lax.rem(lane, CY // 2)

    def strips(groups):
        spots = (
            (0, 8, (lane >= 8) & (lane < 24)),
            (0, 48, (lane >= 32) & (lane < 48)),
            (1, 72, (lane >= 72) & (lane < 88)),
            (1, 112, (lane >= 96) & (lane < 112)),
        )

        def pack(j, values, i, rows, base):
            out = jnp.full((8, CY), base, f32)
            for half, shift, mask in spots:
                out = jnp.where(mask, pltpu.roll(values[half], shift, 1), out)
            before, after = from_l[i, rows, :], from_r[i, rows, :]
            out = jnp.where(in_half < 8, pltpu.roll(before, (CY - 8 * j) % CY, 1) if j else before, out)
            return jnp.where((in_half >= 48) & (in_half < 56), pltpu.roll(after, (CY + 48 - 8 * j) % CY, 1), out)

        for g in groups:
            rows = pl.ds(8 * g, 8)
            padded = pl.ds(PAD + 8 * g, 8)
            for j in range(HALF):
                for i in range(6):
                    source, target = ((ef, se), (hf, sh))[i // 3]
                    values = [source[i % 3, j + HALF * half, padded, :] for half in range(2)]
                    target[i % 3, j, padded, :] = pack(j, values, i, rows, 0.0)
                values = [ids[j + HALF * half, rows, :].astype(f32) for half in range(2)]
                va, vb = lookup(pack(j, values, 6, rows, float(NMAT)))
                strip_a[j, rows, :] = va
                strip_b[j, rows, :] = vb

    def power(bit, carry):
        pr, pi, br, bi = carry
        take = lax.rem(lax.shift_right_logical(ix, bit), 2) == 1
        nr = pr * br - pi * bi
        ni = pr * bi + pi * br
        return (
            jnp.where(take, nr, pr),
            jnp.where(take, ni, pi),
            br * br - bi * bi,
            2.0 * br * bi,
        )

    coefficients(OWN)
    rows_at_once = 8
    for start in range(0, total, rows_at_once):
        part = pl.ds(start, rows_at_once)
        carry = (
            jnp.full((rows_at_once, CY), scale, jnp.float32),
            jnp.zeros((rows_at_once, CY), jnp.float32),
            block.at(0, start, rows_at_once),
            block.at(1, start, rows_at_once),
        )
        for bit in range(max(1, (nx - 1).bit_length())):
            carry = power(bit, carry)
        phase[part, :] = carry[0]
        phase[pl.ds(total + start, rows_at_once), :] = carry[1]
    start_phase = Rows(phase, (0, total))

    await_copies(y_copies)
    strips(OWN)
    await_copies(x_copies)
    strips((0, 3))
    coefficients((0, 3))

    half_x = jnp.where(ix > 0, 0.5, 0.0).astype(f32)
    half_y = jnp.where((in_half < 8) & (iy == 0), 0.0, 0.5).astype(f32)
    on_face = [
        (row + 8 * g >= face[0]) & (row + 8 * g < face[1]) & (lane >= face[2]) & (lane < face[3])
        for g in range(2)
    ]

    def add_sample(n):
        g_re, g_im = (
            jnp.dot(
                sample[...],
                table[pl.ds(starts[part], CY), :],
                precision=lax.Precision.HIGHEST,
                preferred_element_type=jnp.float32,
            )
            for part in range(2)
        )
        ct, st = time.at(0, n, 1), time.at(1, n, 1)
        acc[0] += ct * g_re + st * g_im
        acc[1] += ct * g_im - st * g_re

    def at(g, shift=0):
        return pl.ds(PAD + 8 * g + shift, 8)

    every_group = range(GROUPS)

    def new_magnetic(e, h, z, here, above, factor):
        out = []
        for g in every_group:
            ex, ey, ez = here[g]
            ex_z, ey_z = above[g]
            ey_x, ez_x = e[1, z, at(g, 1), :], e[2, z, at(g, 1), :]
            ex_y, ez_y = pltpu.roll(ex, CY - 1, 1), pltpu.roll(ez, CY - 1, 1)
            hx = h[0, z, at(g), :] - factor[g] * ((ez_y - ez) - (ey_z - ey))
            hy = h[1, z, at(g), :] - factor[g] * ((ex_z - ex) - (ez_x - ez))
            hz = h[2, z, at(g), :] - factor[g] * ((ey_x - ey) - (ex_y - ex))
            h[0, z, at(g), :] = hx
            h[1, z, at(g), :] = hy
            h[2, z, at(g), :] = hz
            out.append((hx, hy, hz))
        return out

    def new_electric(e, h, a, b, z, here, now, below):
        out = []
        for g in every_group:
            ex, ey, ez = here[g]
            hx, hy, hz = now[g]
            hx_z, hy_z = below[g]
            hy_x, hz_x = h[1, z, at(g, -1), :], h[2, z, at(g, -1), :]
            hx_y, hz_y = pltpu.roll(hx, 1, 1), pltpu.roll(hz, 1, 1)
            va, vb = a[z, pl.ds(8 * g, 8), :], b[z, pl.ds(8 * g, 8), :]
            ex = va * ex + vb * ((hz - hz_y) - (hy - hy_z))
            ey = va * ey + vb * ((hx - hx_z) - (hz - hz_x))
            ez = va * ez + vb * ((hy - hy_x) - (hx - hx_y))
            e[0, z, at(g), :] = ex
            e[1, z, at(g), :] = ey
            e[2, z, at(g), :] = ez
            out.append((ex, ey))
        return out

    def plane(e, z):
        return [tuple(e[c, z, at(g), :] for c in range(3)) for g in every_group]

    zero = jnp.zeros((8, CY), f32)
    low_half = lane < CY // 2

    def step(n, carry):
        add_sample(jnp.maximum(n - 1, 0))

        factor = [half_y * (half_x * 2.0)] + [half_y] * 3
        here = first = plane(se, 0)
        below = None
        for j in range(HALF):
            if j < HALF - 1:
                ahead = plane(se, j + 1)
                above = [v[:2] for v in ahead]
            else:
                ahead = None
                above = [
                    tuple(jnp.where(low_half, pltpu.roll(v, CY // 2, 1), 0.0) for v in group[:2]) for group in first
                ]
            now = new_magnetic(se, sh, j, here, above, factor)
            if j:
                new_electric(se, sh, strip_a, strip_b, j, here, now, below)
            else:
                start = now
            below = [v[:2] for v in now]
            here = ahead
        below = [tuple(jnp.where(low_half, 0.0, pltpu.roll(v, CY // 2, 1)) for v in group) for group in below]
        ends = new_electric(se, sh, strip_a, strip_b, 0, plane(se, 0), start, below)
        ends = [ends[g] + start[g][:2] for g in OWN]

        factor = [jnp.full((8, CY), half_x, f32)] + [0.5] * 3
        here = plane(ef, 0)
        below = [(zero, zero)] * GROUPS
        for z in range(NZ):
            if z < NZ - 1:
                ahead = plane(ef, z + 1)
                above = [v[:2] for v in ahead]
            else:
                ahead, above = None, [(zero, zero)] * GROUPS
            now = new_magnetic(ef, hf, z, here, above, factor)
            values = new_electric(ef, hf, coef_a, coef_b, z, here, now, below)
            below = [v[:2] for v in now]
            here = ahead
            if z == ZF:
                for k, g in enumerate(OWN):
                    for c, value in enumerate(values[g] + below[g]):
                        end = ends[k][c]
                        value = jnp.where(lane < 8, pltpu.roll(end, 56, 1), value)
                        value = jnp.where(lane >= CY - 8, pltpu.roll(end, 16, 1), value)
                        sample[pl.ds(c * CX + 8 * k, 8), :] = jnp.where(on_face[k], value, 0.0)
        return carry

    lax.fori_loop(0, STEPS, step, 0)

    add_sample(STEPS - 1)
    outs = []
    for f, (field, strip, out) in enumerate(((ef, se, e_out), (hf, sh, h_out))):
        for c in range(3):
            for z in range(NZ):
                half, j = z // HALF, z % HALF
                for g in OWN:
                    end = strip[c, j, at(g), :]
                    value = field[c, z, at(g), :]
                    value = jnp.where(lane < 8, pltpu.roll(end, (CY - 64 * half - 8) % CY, 1), value)
                    value = jnp.where(lane >= CY - 8, pltpu.roll(end, 80 - 64 * half, 1), value)
                    field[c, z, at(g), :] = value
        copy = pltpu.make_async_copy(field.at[:, :, own_rows], out, out_sem.at[f])
        copy.start()
        outs.append(copy)

    yr, yi = y_start.at(0, iy, 1), y_start.at(1, iy, 1)
    col_re = acc[0] * yr - acc[1] * yi
    acc[1] = acc[0] * yi + acc[1] * yr
    acc[0] = col_re
    for part in range(2):
        for x in range(CX):
            four = acc[part, pl.ds(x, 4, stride=CX), :]
            cols[part, x, pl.ds(0, 4), :] = four
            cols[part, x, pl.ds(4, 4), :] = four

    upper = lax.broadcasted_iota(jnp.int32, (8, CY), 0) < 4
    at_once = min(8, total)

    def send_far(k):
        other = lax.rem(me + k, total)
        return pltpu.make_async_remote_copy(
            src_ref=f_send.at[k],
            dst_ref=f_recv.at[k - 1],
            send_sem=f_send_sem,
            recv_sem=f_recv_sem,
            device_id=(lax.div(other, nx), lax.rem(other, nx)),
            device_id_type=MESH,
        )

    def project(trip, carry):
        k0 = trip * at_once
        picked = [bands[lax.rem(me + k0 + j, total)] for j in range(at_once)]

        def pair(rows, part, j):
            return jnp.where(upper, rows.at(part, picked[j], 1), rows.at(part, picked[j + 1], 1))

        pairs = range(0, at_once, 2)
        wr = [pair(cell, 0, j) for j in pairs]
        wi = [pair(cell, 1, j) for j in pairs]
        c_re, c_im = cols[0, CX - 1], cols[1, CX - 1]
        re = [c_re for _ in pairs]
        im = [c_im for _ in pairs]
        for x in range(CX - 2, -1, -1):
            c_re, c_im = cols[0, x], cols[1, x]
            re, im = (
                [r * a - i * b + c_re for r, i, a, b in zip(re, im, wr, wi)],
                [r * b + i * a + c_im for r, i, a, b in zip(re, im, wr, wi)],
            )
        for t, j in enumerate(pairs):
            pr, pi = pair(start_phase, 0, j), pair(start_phase, 1, j)
            far_re = re[t] * pr - im[t] * pi
            far_im = re[t] * pi + im[t] * pr
            f_send[k0 + j] = jnp.where(upper, far_re, pltpu.roll(far_im, 4, 0))
            f_send[k0 + j + 1] = jnp.where(upper, pltpu.roll(far_re, 4, 0), far_im)
        for j in range(at_once):
            @pl.when(k0 + j > 0)
            def _(j=j):
                send_far(k0 + j).start()
        return carry

    lax.fori_loop(0, total // at_once, project, 0)

    pltpu.make_async_copy(f_recv, f_recv, f_recv_sem).wait()
    if total <= 64:
        terms = [f_send[0]] + [f_recv[k] for k in range(total - 1)]
        while len(terms) > 1:
            terms = [a + b for a, b in zip(terms[::2], terms[1::2])]
        far_out[...] = terms[0]
    else:
        far_out[...] = lax.fori_loop(0, total - 1, lambda k, t: t + f_recv[k], f_send[0])
    pltpu.make_async_copy(f_recv, f_recv, f_send_sem).wait()
    for i, (sends, _, src, dst, device) in enumerate(every):
        @pl.when(sends)
        def _(i=i, src=src, dst=dst, device=device):
            remote(i, src, dst, device).wait_send()
    for copy in outs:
        copy.wait()


def local(ny, nx, electric, magnetic, material_ids, update_ca, update_cb, face_ranges, band_table):
    total = ny * nx
    bands = band_table.shape[0]
    assert bands == total and electric.shape == (3, NZ, CX, CY)
    scale = 1.0 / math.sqrt(CX * nx * CY * ny)
    f32 = jnp.float32
    vmem = pl.BlockSpec(memory_space=pltpu.VMEM)
    hbm = pl.BlockSpec(memory_space=pltpu.HBM)
    packed, starts = tables(bands, ny)
    e_out, h_out, far = pl.pallas_call(
        functools.partial(kernel, ny, nx, scale, starts),
        out_shape=(
            jax.ShapeDtypeStruct(electric.shape, f32),
            jax.ShapeDtypeStruct(electric.shape, f32),
            jax.ShapeDtypeStruct((8, CY), f32),
        ),
        in_specs=[hbm] * 8,
        out_specs=(hbm, hbm, vmem),
        scratch_shapes=[
            pltpu.VMEM((3, NZ, PITCH, CY), f32),
            pltpu.VMEM((3, NZ, PITCH, CY), f32),
            pltpu.VMEM((NZ, ROWS, CY), jnp.int32),
            pltpu.SMEM((NMAT,), f32),
            pltpu.SMEM((NMAT,), f32),
            pltpu.SMEM((4,), jnp.int32),
            pltpu.SMEM((bands,), jnp.int32),
            pltpu.VMEM(packed.shape, f32),
            pltpu.SemaphoreType.DMA((8,)),
            pltpu.VMEM((NZ, ROWS, CY), f32),
            pltpu.VMEM((NZ, ROWS, CY), f32),
            pltpu.VMEM((3, HALF, PITCH, CY), f32),
            pltpu.VMEM((3, HALF, PITCH, CY), f32),
            pltpu.VMEM((HALF, ROWS, CY), f32),
            pltpu.VMEM((HALF, ROWS, CY), f32),
            pltpu.VMEM((7, CX, CY), f32),
            pltpu.VMEM((7, CX, CY), f32),
            pltpu.VMEM((7, ROWS, CY), f32),
            pltpu.VMEM((7, ROWS, CY), f32),
            pltpu.VMEM((4 * CX, CY), f32),
            pltpu.VMEM((2, 4 * CX, CY), f32),
            pltpu.VMEM((2, CX, 8, CY), f32),
            pltpu.VMEM((2 * total, CY), f32),
            pltpu.VMEM((total, 8, CY), f32),
            pltpu.VMEM((total - 1, 8, CY), f32),
            pltpu.SemaphoreType.DMA((12,)),
            pltpu.SemaphoreType.DMA((12,)),
            pltpu.SemaphoreType.DMA,
            pltpu.SemaphoreType.DMA,
            pltpu.SemaphoreType.DMA((2,)),
        ],
        compiler_params=pltpu.CompilerParams(
            collective_id=0, has_side_effects=True, vmem_limit_bytes=62 * 1024 * 1024
        ),
        name="fdtd",
    )(
        electric,
        magnetic,
        material_ids,
        update_ca,
        update_cb,
        face_ranges.reshape(4),
        band_table,
        packed,
    )
    return e_out, h_out, far.reshape(1, 8, CY)


def solution(mesh):
    in_specs = (
        P(None, None, "inner", "grp"),
        P(None, None, "inner", "grp"),
        P(None, "inner", "grp"),
        P(),
        P(),
        P("inner", "grp", None),
        P(),
    )
    out_specs = (
        P(None, None, "inner", "grp"),
        P(None, None, "inner", "grp"),
        P(("grp", "inner"), None, None),
    )
    body = functools.partial(local, mesh.shape["grp"], mesh.shape["inner"])
    return jax.shard_map(body, mesh=mesh, in_specs=in_specs, out_specs=out_specs, check_vma=False)
```

time: 49.7 us -> 54 us (1.087)
  Pallas kernels: 45.8 us -> 50 us
    pallas_call x1, Pallas kernels: 45.8 us -> 50 us  [local(): pl.pallas_call(functools.partial(kernel, ny, nx, scale, starts), out_shap...]
where the time goes in v1:
time: 54 us; the launch traced here: 53.8 us
  Pallas kernels  50 us (93%)
  local copies, waits for them, and re-layouts  3.16 us (6%)
  between operations  0.65 us (1%)
    pallas_call x1, Pallas kernels, local(): pl.pallas_call(functools.partial(kernel, ny, nx, scale, starts), out_shap...  50 us
    unnamed x7, local copies, waits for them, and re-layouts  3.16 us

profile of v1, /device:TPU:0, one launch (start us, length us, event | category | flops | bytes accessed | tf_op | source)
XLA Modules:
  0.0 53.8 jit_solution(15942209135357442551)
XLA Ops:
  0.6 50.0 %fdtd.1 = (f32[3,16,16,128]{3,2,1,0:T(8,128)}, f32[3,16,16,128]{3,2,1,0:T(8,128)}, f32[8,128]{1,0:T(8,128)}) custom-call(f32[3,16,16,128]{3,2,1,0:T(8,128)} %e_hbm.1, f32[3,16,16,128]{3,2,1,0:T(8,128)} %h_hbm.1, s32[16,16,128]{2,1,0:T(8,128)} %ids_hbm.1, f32[8]{0:T(128)} %ca_hbm.1, f32[8]{0:T(128)} %cb_hbm.1, s32[4]{0:T(128)} %bitcast.3, s32[32]{0:T(128)} %bands_hbm.1, ...), custom_call_target="tpu_custom_call" | custom-call | tf_op jit(solution)/shard_map/fdtd/pallas_call | solution.py:516
  50.7 0.0 copy-start
  50.7 1.8 %copy.14 = f32[3,16,16,128]{3,2,1,0:T(8,128)} copy(f32[3,16,16,128]{3,2,1,0:T(8,128)} %get-tuple-element.12) | data formatting | bytes 786432
  52.5 0.0 copy-done
  52.5 0.0 copy-start.1
  52.5 0.7 %copy.15 = f32[3,16,16,128]{3,2,1,0:T(8,128)} copy(f32[3,16,16,128]{3,2,1,0:T(8,128)S(1)} %copy-done) | data formatting | bytes 786432
  53.3 0.0 copy-done.1
  53.3 0.6 %copy.16 = f32[1,8,128]{2,1,0:T(8,128)} copy(f32[1,8,128]{2,1,0:T(8,128)S(1)} %bitcast.2) | data formatting | bytes 8192
Async XLA Ops:
  50.7 1.8 %copy-start = (f32[3,16,16,128]{3,2,1,0:T(8,128)S(1)}, f32[3,16,16,128]{3,2,1,0:T(8,128)}, u32[]{:S(2)}) copy-start(f32[3,16,16,128]{3,2,1,0:T(8,128)} %get-tuple-element.13) | copy-start | bytes 1179652
  52.5 0.8 %copy-start.1 = (f32[8,128]{1,0:T(8,128)S(1)}, f32[8,128]{1,0:T(8,128)}, u32[]{:S(2)}) copy-start(f32[8,128]{1,0:T(8,128)} %get-tuple-element.8) | copy-start | bytes 12292

commit v2 on v1

--- a/solution.py
+++ b/solution.py
@@ -20,11 +20,11 @@
 PAD = 8
 HALO = 8
 ROWS = CX + 2 * HALO
-PITCH = ROWS + 2 * PAD
-GROUPS = ROWS // 8
+GHOST = 4
+PITCH = CX + 2 * PAD
+WIDE = CX + 2 * GHOST + 2 * PAD
 OWN = (1, 2)
 HALF = NZ // 2
-SIDE = CY // 4
 MESH = pl.DeviceIdType.MESH
 
 
@@ -63,11 +63,12 @@
     ny, nx, scale, starts,
     e_hbm, h_hbm, ids_hbm, ca_hbm, cb_hbm, face_hbm, bands_hbm, table_hbm,
     e_out, h_out, far_out,
-    ef, hf, ids, ca, cb, face, bands, table, in_sem,
-    coef_a, coef_b, se, sh, strip_a, strip_b,
+    ef, hf, ids, ca, cb, face, bands, table, e_in, h_in, in_sem,
+    coef_a, coef_b, se, sh, strip_a, strip_b, ce, ch, de, dh,
     edge_r, edge_l, from_l, from_r,
-    sample, acc, cols, phase, f_send, f_recv,
-    send_sem, recv_sem, f_send_sem, f_recv_sem, out_sem,
+    own_h, own_e, left_h, right_e, strip_own_h, strip_own_e, strip_left_h, strip_right_e,
+    samples, strip_samples, sample, acc, cols, phase, f_send, f_recv,
+    send_sem, recv_sem, trace_send, trace_recv, f_send_sem, f_recv_sem, out_sem,
 ):
     iy = lax.axis_index("grp")
     ix = lax.axis_index("inner")
@@ -76,7 +77,7 @@
     f32 = jnp.float32
     lane = lax.broadcasted_iota(jnp.int32, (8, CY), 1)
     row = lax.broadcasted_iota(jnp.int32, (8, CY), 0)
-    own_rows = pl.ds(PAD + HALO, CX)
+    own_rows = pl.ds(PAD, CX)
 
     loads = [
         pltpu.make_async_copy(src, dst, in_sem.at[i])
@@ -90,6 +91,8 @@
                 (face_hbm, face),
                 (bands_hbm, bands),
                 (table_hbm, table),
+                (e_hbm, e_in),
+                (h_hbm, h_in),
             )
         )
     ]
@@ -113,18 +116,41 @@
     low, high = pl.ds(0, 8), pl.ds(8, 8)
     every = (
         (has_yr, has_yl, edge_r, from_l.at[:, pl.ds(HALO, CX)], (iy + 1, ix)),
-        (has_yr & has_xr, has_yl & has_xl, edge_r.at[:, high], from_l.at[:, low], (iy + 1, ix + 1)),
-        (has_yr & has_xl, has_yl & has_xr, edge_r.at[:, low], from_l.at[:, pl.ds(24, 8)], (iy + 1, ix - 1)),
         (has_yl, has_yr, edge_l, from_r.at[:, pl.ds(HALO, CX)], (iy - 1, ix)),
-        (has_yl & has_xr, has_yr & has_xl, edge_l.at[:, high], from_r.at[:, low], (iy - 1, ix + 1)),
-        (has_yl & has_xl, has_yr & has_xr, edge_l.at[:, low], from_r.at[:, pl.ds(24, 8)], (iy - 1, ix - 1)),
-        (has_xr, has_xl, e_hbm.at[:, :, high], ef.at[:, :, pl.ds(PAD, 8)], (iy, ix + 1)),
-        (has_xl, has_xr, e_hbm.at[:, :, low], ef.at[:, :, pl.ds(PAD + 24, 8)], (iy, ix - 1)),
-        (has_xr, has_xl, h_hbm.at[:, :, high], hf.at[:, :, pl.ds(PAD, 8)], (iy, ix + 1)),
-        (has_xl, has_xr, h_hbm.at[:, :, low], hf.at[:, :, pl.ds(PAD + 24, 8)], (iy, ix - 1)),
+        (has_yr & has_xr, has_yl & has_xl, edge_r.at[6, high], from_l.at[6, low], (iy + 1, ix + 1)),
+        (has_yr & has_xl, has_yl & has_xr, edge_r.at[6, low], from_l.at[6, pl.ds(24, 8)], (iy + 1, ix - 1)),
+        (has_yl & has_xr, has_yr & has_xl, edge_l.at[6, high], from_r.at[6, low], (iy - 1, ix + 1)),
+        (has_yl & has_xl, has_yr & has_xr, edge_l.at[6, low], from_r.at[6, pl.ds(24, 8)], (iy - 1, ix - 1)),
         (has_xr, has_xl, ids_hbm.at[:, high], ids.at[:, low], (iy, ix + 1)),
         (has_xl, has_xr, ids_hbm.at[:, low], ids.at[:, pl.ds(24, 8)], (iy, ix - 1)),
     )
+    traces = (
+        (has_xr, has_xl, own_h, left_h, (iy, ix + 1)),
+        (has_xl, has_xr, own_e, right_e, (iy, ix - 1)),
+        (has_xr, has_xl, strip_own_h, strip_left_h, (iy, ix + 1)),
+        (has_xl, has_xr, strip_own_e, strip_right_e, (iy, ix - 1)),
+    )
+
+    def trace(n, k):
+        _, _, src, dst, device = traces[k]
+        return pltpu.make_async_remote_copy(
+            src_ref=src.at[n],
+            dst_ref=dst.at[n],
+            send_sem=trace_send.at[n, k],
+            recv_sem=trace_recv.at[n, k],
+            device_id=device,
+            device_id_type=MESH,
+        )
+
+    def send_trace(n, k):
+        @pl.when(traces[k][0])
+        def _():
+            trace(n, k).start()
+
+    def await_trace(n, k):
+        @pl.when(traces[k][1])
+        def _():
+            trace(n, k).wait_recv()
 
     def remote(i, src, dst, device):
         return pltpu.make_async_remote_copy(
@@ -152,43 +178,33 @@
             def _(i=i, src=src, dst=dst):
                 remote(i, src, dst, (iy, ix)).wait_recv()
 
-    y_copies, x_copies = range(6), range(6, 12)
-
-    for missing, rows in (
-        (jnp.logical_not(has_xl), 0),
-        (jnp.logical_not(has_xr), 24),
-    ):
-        @pl.when(missing)
-        def _(rows=rows):
-            def fill(z, carry):
-                for c in range(3):
-                    ef[c, z, pl.ds(PAD + rows, 8), :] = jnp.zeros((8, CY), f32)
-                    hf[c, z, pl.ds(PAD + rows, 8), :] = jnp.zeros((8, CY), f32)
-                ids[z, pl.ds(rows, 8), :] = jnp.full((8, CY), NMAT, jnp.int32)
-                return carry
-
-            lax.fori_loop(0, NZ, fill, 0)
+    y_copies, x_copies = range(6), range(6, 8)
+
+    for given, rows, arrived in ((has_xl, 0, (left_h, strip_left_h)), (has_xr, 24, (right_e, strip_right_e))):
+        @pl.when(jnp.logical_not(given))
+        def _(rows=rows, arrived=arrived):
+            for buf in arrived:
+                buf[...] = jnp.zeros(buf.shape, f32)
+            ids[:, pl.ds(rows, 8), :] = jnp.full((NZ, 8, CY), NMAT, jnp.int32)
 
     for edge, side in ((from_l, has_yl), (from_r, has_yr)):
+        @pl.when(jnp.logical_not(side))
+        def _(edge=edge):
+            edge[pl.ds(0, 6), pl.ds(HALO, CX), :] = jnp.zeros((6, CX, CY), f32)
+
         for given, rows, count in ((side, 8, 16), (side & has_xl, 0, 8), (side & has_xr, 24, 8)):
             @pl.when(jnp.logical_not(given))
             def _(edge=edge, rows=rows, count=count):
-                edge[pl.ds(0, 6), pl.ds(rows, count), :] = jnp.zeros((6, count, CY), f32)
                 edge[6, pl.ds(rows, count), :] = jnp.full((count, CY), float(NMAT), f32)
 
-    def clear(z, carry):
-        for c in range(3):
-            for rows in (0, PAD + ROWS):
-                ef[c, z, pl.ds(rows, PAD), :] = jnp.zeros((PAD, CY), f32)
-                hf[c, z, pl.ds(rows, PAD), :] = jnp.zeros((PAD, CY), f32)
-        return carry
-
-    lax.fori_loop(0, NZ, clear, 0)
-    for field in (se, sh):
-        for c in range(3):
-            for j in range(HALF):
-                for rows in (0, PAD + ROWS):
-                    field[c, j, pl.ds(rows, PAD), :] = jnp.zeros((PAD, CY), f32)
+    for fields in ((ef, hf), (se, sh)):
+        for field in fields:
+            for c in range(3):
+                for z in range(field.shape[1]):
+                    for rows in (0, PAD + CX):
+                        field[c, z, pl.ds(rows, PAD), :] = jnp.zeros((PAD, CY), f32)
+    for field in (ce, ch, de, dh):
+        field[...] = jnp.zeros(field.shape, f32)
     sample[...] = jnp.zeros(sample.shape, f32)
     acc[...] = jnp.zeros(acc.shape, f32)
 
@@ -202,7 +218,7 @@
             right = jnp.zeros((8, CY), f32)
             left = jnp.zeros((8, CY), f32)
             for z in range(NZ):
-                rows = pl.ds(8 * g + PAD + HALO, 8)
+                rows = pl.ds(8 * g + PAD, 8)
                 if i < 6:
                     value = (ef, hf)[i // 3][i % 3, z, rows, :]
                 else:
@@ -253,11 +269,11 @@
 
         for g in groups:
             rows = pl.ds(8 * g, 8)
-            padded = pl.ds(PAD + 8 * g, 8)
+            padded = pl.ds(PAD + 8 * g - HALO, 8)
             for j in range(HALF):
-                for i in range(6):
-                    source, target = ((ef, se), (hf, sh))[i // 3]
-                    values = [source[i % 3, j + HALF * half, padded, :] for half in range(2)]
+                for i in range(6 if g in OWN else 0):
+                    source, target = ((e_in, se), (h_in, sh))[i // 3]
+                    values = [source[i % 3, j + HALF * half, pl.ds(8 * g - HALO, 8), :] for half in range(2)]
                     target[i % 3, j, padded, :] = pack(j, values, i, rows, 0.0)
                 values = [ids[j + HALF * half, rows, :].astype(f32) for half in range(2)]
                 va, vb = lookup(pack(j, values, 6, rows, float(NMAT)))
@@ -292,13 +308,6 @@
         phase[pl.ds(total + start, rows_at_once), :] = carry[1]
     start_phase = Rows(phase, (0, total))
 
-    await_copies(y_copies)
-    strips(OWN)
-    await_copies(x_copies)
-    strips((0, 3))
-    coefficients((0, 3))
-
-    half_x = jnp.where(ix > 0, 0.5, 0.0).astype(f32)
     half_y = jnp.where((in_half < 8) & (iy == 0), 0.0, 0.5).astype(f32)
     on_face = [
         (row + 8 * g >= face[0]) & (row + 8 * g < face[1]) & (lane >= face[2]) & (lane < face[3])
@@ -322,107 +331,175 @@
     def at(g, shift=0):
         return pl.ds(PAD + 8 * g + shift, 8)
 
-    every_group = range(GROUPS)
-
-    def new_magnetic(e, h, z, here, above, factor):
-        out = []
-        for g in every_group:
+    zero = jnp.zeros((8, CY), f32)
+    low_half = lane < CY // 2
+
+    def new_magnetic(e, h, z, groups, here, above, factor, source):
+        out = {}
+        for g in groups:
             ex, ey, ez = here[g]
             ex_z, ey_z = above[g]
             ey_x, ez_x = e[1, z, at(g, 1), :], e[2, z, at(g, 1), :]
+            if source is not None and g != 1:
+                more_y, more_z = source(g, z)
+                ey_x, ez_x = ey_x + more_y, ez_x + more_z
             ex_y, ez_y = pltpu.roll(ex, CY - 1, 1), pltpu.roll(ez, CY - 1, 1)
-            hx = h[0, z, at(g), :] - factor[g] * ((ez_y - ez) - (ey_z - ey))
-            hy = h[1, z, at(g), :] - factor[g] * ((ex_z - ex) - (ez_x - ez))
-            hz = h[2, z, at(g), :] - factor[g] * ((ey_x - ey) - (ex_y - ex))
+            hx = h[0, z, at(g), :] - factor * ((ez_y - ez) - (ey_z - ey))
+            hy = h[1, z, at(g), :] - factor * ((ex_z - ex) - (ez_x - ez))
+            hz = h[2, z, at(g), :] - factor * ((ey_x - ey) - (ex_y - ex))
             h[0, z, at(g), :] = hx
             h[1, z, at(g), :] = hy
             h[2, z, at(g), :] = hz
-            out.append((hx, hy, hz))
+            out[g] = (hx, hy, hz)
         return out
 
-    def new_electric(e, h, a, b, z, here, now, below):
-        out = []
-        for g in every_group:
+    def new_electric(e, h, a, b, z, groups, base, here, now, below, source):
+        out = {}
+        for g in groups:
             ex, ey, ez = here[g]
             hx, hy, hz = now[g]
             hx_z, hy_z = below[g]
             hy_x, hz_x = h[1, z, at(g, -1), :], h[2, z, at(g, -1), :]
+            if source is not None and g != 1:
+                more_y, more_z = source(g, z)
+                hy_x, hz_x = hy_x + more_y, hz_x + more_z
             hx_y, hz_y = pltpu.roll(hx, 1, 1), pltpu.roll(hz, 1, 1)
-            va, vb = a[z, pl.ds(8 * g, 8), :], b[z, pl.ds(8 * g, 8), :]
+            va, vb = a[z, pl.ds(base + 8 * g, 8), :], b[z, pl.ds(base + 8 * g, 8), :]
             ex = va * ex + vb * ((hz - hz_y) - (hy - hy_z))
             ey = va * ey + vb * ((hx - hx_z) - (hz - hz_x))
             ez = va * ez + vb * ((hy - hy_x) - (hx - hx_y))
             e[0, z, at(g), :] = ex
             e[1, z, at(g), :] = ey
             e[2, z, at(g), :] = ez
-            out.append((ex, ey))
+            out[g] = (ex, ey)
         return out
 
-    def plane(e, z):
-        return [tuple(e[c, z, at(g), :] for c in range(3)) for g in every_group]
-
-    zero = jnp.zeros((8, CY), f32)
-    low_half = lane < CY // 2
-
-    def step(n, carry):
-        add_sample(jnp.maximum(n - 1, 0))
-
-        factor = [half_y * (half_x * 2.0)] + [half_y] * 3
-        here = first = plane(se, 0)
-        below = None
+    def plane(e, z, groups):
+        return {g: tuple(e[c, z, at(g), :] for c in range(3)) for g in groups}
+
+    def two(values):
+        return {g: v[:2] for g, v in values.items()}
+
+    def advance(e, h, groups, base, source_e=None, source_h=None):
+        here = plane(e, 0, groups)
+        nothing = {g: (zero, zero) for g in groups}
+        below = nothing
+        for z in range(NZ):
+            ahead = plane(e, z + 1, groups) if z < NZ - 1 else None
+            above = two(ahead) if ahead else nothing
+            now = new_magnetic(e, h, z, groups, here, above, 0.5, source_e)
+            new_electric(e, h, coef_a, coef_b, z, groups, base, here, now, below, source_h)
+            below, here = two(now), ahead
+
+    def advance_strips(e, h, groups, base, source_e=None, source_h=None):
+        here = first = plane(e, 0, groups)
         for j in range(HALF):
             if j < HALF - 1:
-                ahead = plane(se, j + 1)
-                above = [v[:2] for v in ahead]
+                ahead = plane(e, j + 1, groups)
+                above = two(ahead)
             else:
                 ahead = None
-                above = [
-                    tuple(jnp.where(low_half, pltpu.roll(v, CY // 2, 1), 0.0) for v in group[:2]) for group in first
-                ]
-            now = new_magnetic(se, sh, j, here, above, factor)
+                above = {
+                    g: tuple(jnp.where(low_half, pltpu.roll(v, CY // 2, 1), 0.0) for v in first[g][:2]) for g in groups
+                }
+            now = new_magnetic(e, h, j, groups, here, above, half_y, source_e)
             if j:
-                new_electric(se, sh, strip_a, strip_b, j, here, now, below)
+                new_electric(e, h, strip_a, strip_b, j, groups, base, here, now, below, source_h)
             else:
                 start = now
-            below = [v[:2] for v in now]
-            here = ahead
-        below = [tuple(jnp.where(low_half, 0.0, pltpu.roll(v, CY // 2, 1)) for v in group) for group in below]
-        ends = new_electric(se, sh, strip_a, strip_b, 0, plane(se, 0), start, below)
-        ends = [ends[g] + start[g][:2] for g in OWN]
-
-        factor = [jnp.full((8, CY), half_x, f32)] + [0.5] * 3
-        here = plane(ef, 0)
-        below = [(zero, zero)] * GROUPS
-        for z in range(NZ):
-            if z < NZ - 1:
-                ahead = plane(ef, z + 1)
-                above = [v[:2] for v in ahead]
-            else:
-                ahead, above = None, [(zero, zero)] * GROUPS
-            now = new_magnetic(ef, hf, z, here, above, factor)
-            values = new_electric(ef, hf, coef_a, coef_b, z, here, now, below)
-            below = [v[:2] for v in now]
-            here = ahead
-            if z == ZF:
-                for k, g in enumerate(OWN):
-                    for c, value in enumerate(values[g] + below[g]):
-                        end = ends[k][c]
-                        value = jnp.where(lane < 8, pltpu.roll(end, 56, 1), value)
-                        value = jnp.where(lane >= CY - 8, pltpu.roll(end, 16, 1), value)
-                        sample[pl.ds(c * CX + 8 * k, 8), :] = jnp.where(on_face[k], value, 0.0)
+            below, here = two(now), ahead
+        below = {g: tuple(jnp.where(low_half, 0.0, pltpu.roll(v, CY // 2, 1)) for v in below[g]) for g in groups}
+        new_electric(e, h, strip_a, strip_b, 0, groups, base, plane(e, 0, groups), start, below, source_h)
+
+    def borders(n, e, h, mine_e, mine_h, run, k):
+        depth = e.shape[1]
+        for c in (1, 2):
+            mine_e[n, pl.ds((c - 1) * depth, depth), :] = e[c, :, PAD, :]
+        send_trace(n, k + 1)
+        run(e, h, (0, 1), HALO)
+        for c in (1, 2):
+            mine_h[n, pl.ds((c - 1) * depth, depth), :] = h[c, :, PAD + CX - 1, :]
+        send_trace(n, k)
+
+    def keep(n, e, h, z, kept, first_row, add):
+        for c, (field, part) in enumerate(((e, 0), (e, 1), (h, 0), (h, 1))):
+            for k in range(2):
+                spot = pl.ds(c * CX + 8 * k, 8)
+                value = field[part, z, pl.ds(first_row + 8 * k, 8), :]
+                kept[n, spot, :] = kept[n, spot, :] + value if add else value
+
+    def alone(n, carry):
+        borders(n, ef, hf, own_e, own_h, advance, 0)
+        keep(n, ef, hf, ZF, samples, PAD, False)
         return carry
 
-    lax.fori_loop(0, STEPS, step, 0)
+    def alone_strips(n, carry):
+        borders(n, se, sh, strip_own_e, strip_own_h, advance_strips, 2)
+        keep(n, se, sh, 0, strip_samples, PAD, False)
+        return carry
+
+    def sources(n, left, right, spot, depth):
+        masks = {0: (row == spot) & has_xl, 2: row == spot}
+
+        def source(g, z):
+            buf = left if g == 0 else right
+            return tuple(
+                jnp.where(masks[g], jnp.broadcast_to(buf[n, pl.ds(c * depth + z, 1), :], (8, CY)), 0.0) for c in range(2)
+            )
+
+        return source
+
+    SHIFT = HALO - GHOST
+
+    def correct(groups, n, carry):
+        await_trace(n, 0)
+        await_trace(n, 1)
+        advance(
+            ce, ch, groups, SHIFT,
+            sources(n, own_e, right_e, GHOST - 1, NZ), sources(n, left_h, own_h, GHOST, NZ),
+        )
+        keep(n, ce, ch, ZF, samples, PAD + GHOST, True)
+        return carry
+
+    def correct_strips(groups, n, carry):
+        add_sample(jnp.maximum(n - 1, 0))
+        await_trace(n, 2)
+        await_trace(n, 3)
+        advance_strips(
+            de, dh, groups, SHIFT,
+            sources(n, strip_own_e, strip_right_e, GHOST - 1, HALF), sources(n, strip_left_h, strip_own_h, GHOST, HALF),
+        )
+        keep(n, de, dh, 0, strip_samples, PAD + GHOST, True)
+        for c in range(4):
+            for k in range(2):
+                spot = pl.ds(c * CX + 8 * k, 8)
+                end = strip_samples[n, spot, :]
+                value = jnp.where(lane < 8, pltpu.roll(end, 56, 1), samples[n, spot, :])
+                value = jnp.where(lane >= CY - 8, pltpu.roll(end, 16, 1), value)
+                sample[spot, :] = jnp.where(on_face[k], value, 0.0)
+        return carry
+
+    lax.fori_loop(0, STEPS, alone, 0)
+    await_copies(y_copies)
+    strips(OWN)
+    lax.fori_loop(0, STEPS, alone_strips, 0)
+    await_copies(x_copies)
+    strips((0, 3))
+    coefficients((0, 3))
+    lax.fori_loop(0, STEPS // 2, functools.partial(correct, (0, 2)), 0)
+    lax.fori_loop(STEPS // 2, STEPS, functools.partial(correct, (0, 1, 2)), 0)
+    lax.fori_loop(0, STEPS // 2, functools.partial(correct_strips, (0, 2)), 0)
+    lax.fori_loop(STEPS // 2, STEPS, functools.partial(correct_strips, (0, 1, 2)), 0)
 
     add_sample(STEPS - 1)
     outs = []
-    for f, (field, strip, out) in enumerate(((ef, se, e_out), (hf, sh, h_out))):
+    for f, (field, strip, more, strip_more, out) in enumerate(((ef, se, ce, de, e_out), (hf, sh, ch, dh, h_out))):
         for c in range(3):
             for z in range(NZ):
                 half, j = z // HALF, z % HALF
-                for g in OWN:
-                    end = strip[c, j, at(g), :]
-                    value = field[c, z, at(g), :]
+                for g in range(2):
+                    end = strip[c, j, at(g), :] + strip_more[c, j, at(g, GHOST), :]
+                    value = field[c, z, at(g), :] + more[c, z, at(g, GHOST), :]
                     value = jnp.where(lane < 8, pltpu.roll(end, (CY - 64 * half - 8) % CY, 1), value)
                     value = jnp.where(lane >= CY - 8, pltpu.roll(end, 80 - 64 * half, 1), value)
                     field[c, z, at(g), :] = value
@@ -500,6 +577,15 @@
         @pl.when(sends)
         def _(i=i, src=src, dst=dst, device=device):
             remote(i, src, dst, device).wait_send()
+
+    def sent(n, carry):
+        for k in range(4):
+            @pl.when(traces[k][0])
+            def _(k=k):
+                trace(n, k).wait_send()
+        return carry
+
+    lax.fori_loop(0, STEPS, sent, 0)
     for copy in outs:
         copy.wait()
 
@@ -531,25 +617,37 @@
             pltpu.SMEM((4,), jnp.int32),
             pltpu.SMEM((bands,), jnp.int32),
             pltpu.VMEM(packed.shape, f32),
-            pltpu.SemaphoreType.DMA((8,)),
+            pltpu.VMEM((3, NZ, CX, CY), f32),
+            pltpu.VMEM((3, NZ, CX, CY), f32),
+            pltpu.SemaphoreType.DMA((10,)),
             pltpu.VMEM((NZ, ROWS, CY), f32),
             pltpu.VMEM((NZ, ROWS, CY), f32),
             pltpu.VMEM((3, HALF, PITCH, CY), f32),
             pltpu.VMEM((3, HALF, PITCH, CY), f32),
             pltpu.VMEM((HALF, ROWS, CY), f32),
             pltpu.VMEM((HALF, ROWS, CY), f32),
+            pltpu.VMEM((3, NZ, WIDE, CY), f32),
+            pltpu.VMEM((3, NZ, WIDE, CY), f32),
+            pltpu.VMEM((3, HALF, WIDE, CY), f32),
+            pltpu.VMEM((3, HALF, WIDE, CY), f32),
             pltpu.VMEM((7, CX, CY), f32),
             pltpu.VMEM((7, CX, CY), f32),
             pltpu.VMEM((7, ROWS, CY), f32),
             pltpu.VMEM((7, ROWS, CY), f32),
+            *[pltpu.VMEM((STEPS, 2 * NZ, CY), f32)] * 4,
+            *[pltpu.VMEM((STEPS, 2 * HALF, CY), f32)] * 4,
+            pltpu.VMEM((STEPS, 4 * CX, CY), f32),
+            pltpu.VMEM((STEPS, 4 * CX, CY), f32),
             pltpu.VMEM((4 * CX, CY), f32),
             pltpu.VMEM((2, 4 * CX, CY), f32),
             pltpu.VMEM((2, CX, 8, CY), f32),
             pltpu.VMEM((2 * total, CY), f32),
             pltpu.VMEM((total, 8, CY), f32),
             pltpu.VMEM((total - 1, 8, CY), f32),
-            pltpu.SemaphoreType.DMA((12,)),
-            pltpu.SemaphoreType.DMA((12,)),
+            pltpu.SemaphoreType.DMA((8,)),
+            pltpu.SemaphoreType.DMA((8,)),
+            pltpu.SemaphoreType.DMA((STEPS, 4)),
+            pltpu.SemaphoreType.DMA((STEPS, 4)),
             pltpu.SemaphoreType.DMA,
             pltpu.SemaphoreType.DMA,
             pltpu.SemaphoreType.DMA((2,)),

time: 54 us -> 36 us (0.67)
  Pallas kernels: 50 us -> 32 us
    pallas_call x1, Pallas kernels: 50 us -> 32 us  [local(): pl.pallas_call(functools.partial(kernel, ny, nx, scale, starts), out_shap...]
where the time goes in v2:
time: 36 us; the launch traced here: 35.8 us
  Pallas kernels  32 us (89%)
  local copies, waits for them, and re-layouts  3.16 us (9%)
  between operations  0.65 us (2%)
    pallas_call x1, Pallas kernels, local(): pl.pallas_call(functools.partial(kernel, ny, nx, scale, starts), out_shap...  32 us
    unnamed x7, local copies, waits for them, and re-layouts  3.16 us

profile of v2, /device:TPU:0, one launch (start us, length us, event | category | flops | bytes accessed | tf_op | source)
XLA Modules:
  0.0 35.8 jit_solution(13304238755881669333)
XLA Ops:
  0.6 32.0 %fdtd.1 = (f32[3,16,16,128]{3,2,1,0:T(8,128)}, f32[3,16,16,128]{3,2,1,0:T(8,128)}, f32[8,128]{1,0:T(8,128)}) custom-call(f32[3,16,16,128]{3,2,1,0:T(8,128)} %e_hbm.1, f32[3,16,16,128]{3,2,1,0:T(8,128)} %h_hbm.1, s32[16,16,128]{2,1,0:T(8,128)} %ids_hbm.1, f32[8]{0:T(128)} %ca_hbm.1, f32[8]{0:T(128)} %cb_hbm.1, s32[4]{0:T(128)} %bitcast.3, s32[32]{0:T(128)} %bands_hbm.1, ...), custom_call_target="tpu_custom_call" | custom-call | tf_op jit(solution)/shard_map/fdtd/pallas_call | solution.py:602
  32.7 0.0 copy-start
  32.7 1.8 %copy.14 = f32[3,16,16,128]{3,2,1,0:T(8,128)} copy(f32[3,16,16,128]{3,2,1,0:T(8,128)} %get-tuple-element.12) | data formatting | bytes 786432
  34.5 0.0 copy-done
  34.5 0.0 copy-start.1
  34.5 0.7 %copy.15 = f32[3,16,16,128]{3,2,1,0:T(8,128)} copy(f32[3,16,16,128]{3,2,1,0:T(8,128)S(1)} %copy-done) | data formatting | bytes 786432
  35.2 0.0 copy-done.1
  35.2 0.6 %copy.16 = f32[1,8,128]{2,1,0:T(8,128)} copy(f32[1,8,128]{2,1,0:T(8,128)S(1)} %bitcast.2) | data formatting | bytes 8192
Async XLA Ops:
  32.7 1.8 %copy-start = (f32[3,16,16,128]{3,2,1,0:T(8,128)S(1)}, f32[3,16,16,128]{3,2,1,0:T(8,128)}, u32[]{:S(2)}) copy-start(f32[3,16,16,128]{3,2,1,0:T(8,128)} %get-tuple-element.13) | copy-start | bytes 1179652
  34.5 0.8 %copy-start.1 = (f32[8,128]{1,0:T(8,128)S(1)}, f32[8,128]{1,0:T(8,128)}, u32[]{:S(2)}) copy-start(f32[8,128]{1,0:T(8,128)} %get-tuple-element.8) | copy-start | bytes 12292

commit v3 on v2

--- a/solution.py
+++ b/solution.py
@@ -51,6 +51,17 @@
     return packed, tuple(int(start) for start in starts[:-1])
 
 
+def round_offsets(ny, nx):
+    rounds, reach = [], 1
+    while reach < max(ny, nx) - 1:
+        rounds.append(
+            [(0, s * reach) for s in (-1, 1) if reach < nx - 1] + [(s * reach, 0) for s in (-1, 1) if reach < ny - 1]
+        )
+        reach *= 2
+    rounds.append([(s * d, 0) for d in range(1, ny) for s in (-1, 1)])
+    return rounds
+
+
 class Rows:
     def __init__(self, ref, starts):
         self.ref, self.starts = ref, starts
@@ -65,10 +76,10 @@
     e_out, h_out, far_out,
     ef, hf, ids, ca, cb, face, bands, table, e_in, h_in, in_sem,
     coef_a, coef_b, se, sh, strip_a, strip_b, ce, ch, de, dh,
-    edge_r, edge_l, from_l, from_r,
+    edge_r, edge_l, from_l, from_r, last_ids, first_ids, left_ids, right_ids,
     own_h, own_e, left_h, right_e, strip_own_h, strip_own_e, strip_left_h, strip_right_e,
-    samples, strip_samples, sample, acc, cols, phase, f_send, f_recv,
-    send_sem, recv_sem, trace_send, trace_recv, f_send_sem, f_recv_sem, out_sem,
+    samples, strip_samples, sample, turned, acc, cols, phase, f_send, f_recv,
+    send_sem, recv_sem, trace_send, trace_recv, round_sem, f_send_sem, f_recv_sem, out_sem,
 ):
     iy = lax.axis_index("grp")
     ix = lax.axis_index("inner")
@@ -102,17 +113,33 @@
 
     barrier = pltpu.get_barrier_semaphore()
 
-    def greet(k, carry):
-        other = lax.rem(me + k, total)
-        pl.semaphore_signal(
-            barrier, inc=1, device_id=(lax.div(other, nx), lax.rem(other, nx)), device_id_type=MESH
-        )
-        return carry
-
-    lax.fori_loop(1, total, greet, 0)
-
     has_xr, has_xl = ix < nx - 1, ix > 0
     has_yr, has_yl = iy < ny - 1, iy > 0
+
+    def within(y, x):
+        return (y >= 0) & (y < ny) & (x >= 0) & (x < nx)
+
+    def signal_all(sem, offsets):
+        for dy, dx in offsets:
+            @pl.when(within(iy + dy, ix + dx))
+            def _(dy=dy, dx=dx):
+                pl.semaphore_signal(sem, inc=1, device_id=(iy + dy, ix + dx), device_id_type=MESH)
+
+    def partners(offsets):
+        return sum(jnp.where(within(iy + dy, ix + dx), 1, 0) for dy, dx in offsets)
+
+    around = [(dy, dx) for dy in (-1, 0, 1) for dx in (-1, 0, 1) if (dy, dx) != (0, 0)]
+    signal_all(barrier, around)
+    rounds = round_offsets(ny, nx)
+
+    def begin_round(k):
+        if k > 0:
+            end_round(k - 1)
+        signal_all(round_sem.at[k], rounds[k])
+
+    def end_round(k):
+        pl.semaphore_wait(round_sem.at[k], partners(rounds[k]))
+
     low, high = pl.ds(0, 8), pl.ds(8, 8)
     every = (
         (has_yr, has_yl, edge_r, from_l.at[:, pl.ds(HALO, CX)], (iy + 1, ix)),
@@ -121,8 +148,8 @@
         (has_yr & has_xl, has_yl & has_xr, edge_r.at[6, low], from_l.at[6, pl.ds(24, 8)], (iy + 1, ix - 1)),
         (has_yl & has_xr, has_yr & has_xl, edge_l.at[6, high], from_r.at[6, low], (iy - 1, ix + 1)),
         (has_yl & has_xl, has_yr & has_xr, edge_l.at[6, low], from_r.at[6, pl.ds(24, 8)], (iy - 1, ix - 1)),
-        (has_xr, has_xl, ids_hbm.at[:, high], ids.at[:, low], (iy, ix + 1)),
-        (has_xl, has_xr, ids_hbm.at[:, low], ids.at[:, pl.ds(24, 8)], (iy, ix - 1)),
+        (has_xr, has_xl, last_ids, left_ids, (iy, ix + 1)),
+        (has_xl, has_xr, first_ids, right_ids, (iy, ix - 1)),
     )
     traces = (
         (has_xr, has_xl, own_h, left_h, (iy, ix + 1)),
@@ -178,14 +205,14 @@
             def _(i=i, src=src, dst=dst):
                 remote(i, src, dst, (iy, ix)).wait_recv()
 
-    y_copies, x_copies = range(6), range(6, 8)
-
-    for given, rows, arrived in ((has_xl, 0, (left_h, strip_left_h)), (has_xr, 24, (right_e, strip_right_e))):
+    y_copies, corner_copies, x_copies = range(2), range(2, 6), range(6, 8)
+
+    for given, fresh, arrived in ((has_xl, left_ids, (left_h, strip_left_h)), (has_xr, right_ids, (right_e, strip_right_e))):
         @pl.when(jnp.logical_not(given))
-        def _(rows=rows, arrived=arrived):
+        def _(fresh=fresh, arrived=arrived):
             for buf in arrived:
                 buf[...] = jnp.zeros(buf.shape, f32)
-            ids[:, pl.ds(rows, 8), :] = jnp.full((NZ, 8, CY), NMAT, jnp.int32)
+            fresh[...] = jnp.full(fresh.shape, NMAT, jnp.int32)
 
     for edge, side in ((from_l, has_yl), (from_r, has_yr)):
         @pl.when(jnp.logical_not(side))
@@ -203,16 +230,21 @@
                 for z in range(field.shape[1]):
                     for rows in (0, PAD + CX):
                         field[c, z, pl.ds(rows, PAD), :] = jnp.zeros((PAD, CY), f32)
+    ids[:, pl.ds(0, 8), :] = jnp.full((NZ, 8, CY), NMAT, jnp.int32)
+    ids[:, pl.ds(HALO + CX, 8), :] = jnp.full((NZ, 8, CY), NMAT, jnp.int32)
     for field in (ce, ch, de, dh):
         field[...] = jnp.zeros(field.shape, f32)
-    sample[...] = jnp.zeros(sample.shape, f32)
-    acc[...] = jnp.zeros(acc.shape, f32)
-
-    pl.semaphore_wait(barrier, total - 1)
-    start_copies(x_copies)
+
+    pl.semaphore_wait(barrier, partners(around))
+    begin_round(0)
     for load in loads:
         load.wait()
 
+    for z in range(NZ):
+        spot = pl.ds(z * GHOST, GHOST)
+        last_ids[spot, :] = ids[z, pl.ds(HALO + CX - GHOST, GHOST), :]
+        first_ids[spot, :] = ids[z, pl.ds(HALO, GHOST), :]
+    start_copies(x_copies)
     for i in range(7):
         for g in range(2):
             right = jnp.zeros((8, CY), f32)
@@ -229,6 +261,7 @@
             edge_r[i, pl.ds(8 * g, 8), :] = right
             edge_l[i, pl.ds(8 * g, 8), :] = left
     start_copies(y_copies)
+    start_copies(corner_copies)
 
     def lookup(here):
         va = jnp.zeros((8, CY), f32)
@@ -313,20 +346,6 @@
         (row + 8 * g >= face[0]) & (row + 8 * g < face[1]) & (lane >= face[2]) & (lane < face[3])
         for g in range(2)
     ]
-
-    def add_sample(n):
-        g_re, g_im = (
-            jnp.dot(
-                sample[...],
-                table[pl.ds(starts[part], CY), :],
-                precision=lax.Precision.HIGHEST,
-                preferred_element_type=jnp.float32,
-            )
-            for part in range(2)
-        )
-        ct, st = time.at(0, n, 1), time.at(1, n, 1)
-        acc[0] += ct * g_re + st * g_im
-        acc[1] += ct * g_im - st * g_re
 
     def at(g, shift=0):
         return pl.ds(PAD + 8 * g + shift, 8)
@@ -461,52 +480,71 @@
         keep(n, ce, ch, ZF, samples, PAD + GHOST, True)
         return carry
 
-    def correct_strips(groups, n, carry):
-        add_sample(jnp.maximum(n - 1, 0))
-        await_trace(n, 2)
-        await_trace(n, 3)
+    def correct_strips(groups, n):
         advance_strips(
             de, dh, groups, SHIFT,
             sources(n, strip_own_e, strip_right_e, GHOST - 1, HALF), sources(n, strip_left_h, strip_own_h, GHOST, HALF),
         )
         keep(n, de, dh, 0, strip_samples, PAD + GHOST, True)
+
+    def correct_both(strip_groups, i, carry):
+        n = STEPS // 2 + i
+        await_trace(2 * i, 2)
+        await_trace(2 * i, 3)
+        await_trace(2 * i + 1, 2)
+        await_trace(2 * i + 1, 3)
+        correct((0, 1, 2), n, carry)
+        correct_strips(strip_groups, 2 * i)
+        correct_strips(strip_groups, 2 * i + 1)
+        return carry
+
+    lax.fori_loop(0, STEPS, alone, 0)
+    begin_round(1)
+    await_copies(y_copies)
+    strips(OWN)
+    lax.fori_loop(0, STEPS, alone_strips, 0)
+    begin_round(2)
+    await_copies(x_copies)
+    await_copies(corner_copies)
+    for z in range(NZ):
+        spot = pl.ds(z * GHOST, GHOST)
+        ids[z, pl.ds(HALO - GHOST, GHOST), :] = left_ids[spot, :]
+        ids[z, pl.ds(HALO + CX, GHOST), :] = right_ids[spot, :]
+    strips((0, 3))
+    coefficients((0, 3))
+    lax.fori_loop(0, STEPS // 2, functools.partial(correct, (0, 2)), 0)
+    lax.fori_loop(0, STEPS // 4, functools.partial(correct_both, (0, 2)), 0)
+    begin_round(3)
+    lax.fori_loop(STEPS // 4, STEPS // 2, functools.partial(correct_both, (0, 1, 2)), 0)
+
+    for k in range(4, len(rounds)):
+        begin_round(k)
+    for n in range(STEPS):
         for c in range(4):
             for k in range(2):
                 spot = pl.ds(c * CX + 8 * k, 8)
                 end = strip_samples[n, spot, :]
                 value = jnp.where(lane < 8, pltpu.roll(end, 56, 1), samples[n, spot, :])
                 value = jnp.where(lane >= CY - 8, pltpu.roll(end, 16, 1), value)
-                sample[spot, :] = jnp.where(on_face[k], value, 0.0)
-        return carry
-
-    lax.fori_loop(0, STEPS, alone, 0)
-    await_copies(y_copies)
-    strips(OWN)
-    lax.fori_loop(0, STEPS, alone_strips, 0)
-    await_copies(x_copies)
-    strips((0, 3))
-    coefficients((0, 3))
-    lax.fori_loop(0, STEPS // 2, functools.partial(correct, (0, 2)), 0)
-    lax.fori_loop(STEPS // 2, STEPS, functools.partial(correct, (0, 1, 2)), 0)
-    lax.fori_loop(0, STEPS // 2, functools.partial(correct_strips, (0, 2)), 0)
-    lax.fori_loop(STEPS // 2, STEPS, functools.partial(correct_strips, (0, 1, 2)), 0)
-
-    add_sample(STEPS - 1)
-    outs = []
-    for f, (field, strip, more, strip_more, out) in enumerate(((ef, se, ce, de, e_out), (hf, sh, ch, dh, h_out))):
-        for c in range(3):
-            for z in range(NZ):
-                half, j = z // HALF, z % HALF
-                for g in range(2):
-                    end = strip[c, j, at(g), :] + strip_more[c, j, at(g, GHOST), :]
-                    value = field[c, z, at(g), :] + more[c, z, at(g, GHOST), :]
-                    value = jnp.where(lane < 8, pltpu.roll(end, (CY - 64 * half - 8) % CY, 1), value)
-                    value = jnp.where(lane >= CY - 8, pltpu.roll(end, 80 - 64 * half, 1), value)
-                    field[c, z, at(g), :] = value
-        copy = pltpu.make_async_copy(field.at[:, :, own_rows], out, out_sem.at[f])
-        copy.start()
-        outs.append(copy)
-
+                sample[pl.ds(n * 4 * CX + c * CX + 8 * k, 8), :] = jnp.where(on_face[k], value, 0.0)
+    for part in range(2):
+        turned[part] = jnp.dot(
+            sample[...],
+            table[pl.ds(starts[part], CY), :],
+            precision=lax.Precision.HIGHEST,
+            preferred_element_type=f32,
+        )
+    for first in range(0, 4 * CX, 8):
+        re, im = zero, zero
+        for n in range(STEPS):
+            g_re, g_im = (turned[part, pl.ds(n * 4 * CX + first, 8), :] for part in range(2))
+            ct, st = time.at(0, n, 1), time.at(1, n, 1)
+            re += ct * g_re + st * g_im
+            im += ct * g_im - st * g_re
+        acc[0, pl.ds(first, 8), :] = re
+        acc[1, pl.ds(first, 8), :] = im
+
+    end_round(len(rounds) - 1)
     yr, yi = y_start.at(0, iy, 1), y_start.at(1, iy, 1)
     col_re = acc[0] * yr - acc[1] * yi
     acc[1] = acc[0] * yi + acc[1] * yr
@@ -563,6 +601,21 @@
         return carry
 
     lax.fori_loop(0, total // at_once, project, 0)
+
+    outs = []
+    for f, (field, strip, more, strip_more, out) in enumerate(((ef, se, ce, de, e_out), (hf, sh, ch, dh, h_out))):
+        for c in range(3):
+            for z in range(NZ):
+                half, j = z // HALF, z % HALF
+                for g in range(2):
+                    end = strip[c, j, at(g), :] + strip_more[c, j, at(g, GHOST), :]
+                    value = field[c, z, at(g), :] + more[c, z, at(g, GHOST), :]
+                    value = jnp.where(lane < 8, pltpu.roll(end, (CY - 64 * half - 8) % CY, 1), value)
+                    value = jnp.where(lane >= CY - 8, pltpu.roll(end, 80 - 64 * half, 1), value)
+                    field[c, z, at(g), :] = value
+        copy = pltpu.make_async_copy(field.at[:, :, own_rows], out, out_sem.at[f])
+        copy.start()
+        outs.append(copy)
 
     pltpu.make_async_copy(f_recv, f_recv, f_recv_sem).wait()
     if total <= 64:
@@ -634,11 +687,13 @@
             pltpu.VMEM((7, CX, CY), f32),
             pltpu.VMEM((7, ROWS, CY), f32),
             pltpu.VMEM((7, ROWS, CY), f32),
+            *[pltpu.VMEM((NZ * GHOST, CY), jnp.int32)] * 4,
             *[pltpu.VMEM((STEPS, 2 * NZ, CY), f32)] * 4,
             *[pltpu.VMEM((STEPS, 2 * HALF, CY), f32)] * 4,
             pltpu.VMEM((STEPS, 4 * CX, CY), f32),
             pltpu.VMEM((STEPS, 4 * CX, CY), f32),
-            pltpu.VMEM((4 * CX, CY), f32),
+            pltpu.VMEM((STEPS * 4 * CX, CY), f32),
+            pltpu.VMEM((2, STEPS * 4 * CX, CY), f32),
             pltpu.VMEM((2, 4 * CX, CY), f32),
             pltpu.VMEM((2, CX, 8, CY), f32),
             pltpu.VMEM((2 * total, CY), f32),
@@ -648,6 +703,7 @@
             pltpu.SemaphoreType.DMA((8,)),
             pltpu.SemaphoreType.DMA((STEPS, 4)),
             pltpu.SemaphoreType.DMA((STEPS, 4)),
+            pltpu.SemaphoreType.REGULAR((len(round_offsets(ny, nx)),)),
             pltpu.SemaphoreType.DMA,
             pltpu.SemaphoreType.DMA,
             pltpu.SemaphoreType.DMA((2,)),

time: 36 us -> 34 us (0.944)
  Pallas kernels: 32 us -> 30 us
    pallas_call x1, Pallas kernels: 32 us -> 30 us  [local(): pl.pallas_call(functools.partial(kernel, ny, nx, scale, starts), out_shap...]
where the time goes in v3:
time: 34 us; the launch traced here: 33.8 us
  Pallas kernels  30 us (88%)
  local copies, waits for them, and re-layouts  3.16 us (9%)
  between operations  0.65 us (2%)
    pallas_call x1, Pallas kernels, local(): pl.pallas_call(functools.partial(kernel, ny, nx, scale, starts), out_shap...  30 us
    unnamed x7, local copies, waits for them, and re-layouts  3.16 us

profile of v3, /device:TPU:0, one launch (start us, length us, event | category | flops | bytes accessed | tf_op | source)
XLA Modules:
  0.0 33.8 jit_solution(4475112254388937191)
XLA Ops:
  0.6 30.0 %fdtd.1 = (f32[3,16,16,128]{3,2,1,0:T(8,128)}, f32[3,16,16,128]{3,2,1,0:T(8,128)}, f32[8,128]{1,0:T(8,128)}) custom-call(f32[3,16,16,128]{3,2,1,0:T(8,128)} %e_hbm.1, f32[3,16,16,128]{3,2,1,0:T(8,128)} %h_hbm.1, s32[16,16,128]{2,1,0:T(8,128)} %ids_hbm.1, f32[8]{0:T(128)} %ca_hbm.1, f32[8]{0:T(128)} %cb_hbm.1, s32[4]{0:T(128)} %bitcast.3, s32[32]{0:T(128)} %bands_hbm.1, ...), custom_call_target="tpu_custom_call" | custom-call | tf_op jit(solution)/shard_map/fdtd/pallas_call | solution.py:655
  30.6 0.0 copy-start
  30.7 1.8 %copy.14 = f32[3,16,16,128]{3,2,1,0:T(8,128)} copy(f32[3,16,16,128]{3,2,1,0:T(8,128)} %get-tuple-element.12) | data formatting | bytes 786432
  32.5 0.0 copy-done
  32.5 0.0 copy-start.1
  32.5 0.7 %copy.15 = f32[3,16,16,128]{3,2,1,0:T(8,128)} copy(f32[3,16,16,128]{3,2,1,0:T(8,128)S(1)} %copy-done) | data formatting | bytes 786432
  33.2 0.0 copy-done.1
  33.2 0.6 %copy.16 = f32[1,8,128]{2,1,0:T(8,128)} copy(f32[1,8,128]{2,1,0:T(8,128)S(1)} %bitcast.2) | data formatting | bytes 8192
Async XLA Ops:
  30.6 1.8 %copy-start = (f32[3,16,16,128]{3,2,1,0:T(8,128)S(1)}, f32[3,16,16,128]{3,2,1,0:T(8,128)}, u32[]{:S(2)}) copy-start(f32[3,16,16,128]{3,2,1,0:T(8,128)} %get-tuple-element.13) | copy-start | bytes 1179652
  32.5 0.8 %copy-start.1 = (f32[8,128]{1,0:T(8,128)S(1)}, f32[8,128]{1,0:T(8,128)}, u32[]{:S(2)}) copy-start(f32[8,128]{1,0:T(8,128)} %get-tuple-element.8) | copy-start | bytes 12292

commit v4 on v3

--- a/solution.py
+++ b/solution.py
@@ -79,7 +79,7 @@
     edge_r, edge_l, from_l, from_r, last_ids, first_ids, left_ids, right_ids,
     own_h, own_e, left_h, right_e, strip_own_h, strip_own_e, strip_left_h, strip_right_e,
     samples, strip_samples, sample, turned, acc, cols, phase, f_send, f_recv,
-    send_sem, recv_sem, trace_send, trace_recv, round_sem, f_send_sem, f_recv_sem, out_sem,
+    send_sem, recv_sem, trace_send, trace_recv, round_sem, f_send_sem, f_recv_sem,
 ):
     iy = lax.axis_index("grp")
     ix = lax.axis_index("inner")
@@ -480,22 +480,14 @@
         keep(n, ce, ch, ZF, samples, PAD + GHOST, True)
         return carry
 
-    def correct_strips(groups, n):
+    def correct_strips(groups, n, carry):
+        await_trace(n, 2)
+        await_trace(n, 3)
         advance_strips(
             de, dh, groups, SHIFT,
             sources(n, strip_own_e, strip_right_e, GHOST - 1, HALF), sources(n, strip_left_h, strip_own_h, GHOST, HALF),
         )
         keep(n, de, dh, 0, strip_samples, PAD + GHOST, True)
-
-    def correct_both(strip_groups, i, carry):
-        n = STEPS // 2 + i
-        await_trace(2 * i, 2)
-        await_trace(2 * i, 3)
-        await_trace(2 * i + 1, 2)
-        await_trace(2 * i + 1, 3)
-        correct((0, 1, 2), n, carry)
-        correct_strips(strip_groups, 2 * i)
-        correct_strips(strip_groups, 2 * i + 1)
         return carry
 
     lax.fori_loop(0, STEPS, alone, 0)
@@ -513,9 +505,10 @@
     strips((0, 3))
     coefficients((0, 3))
     lax.fori_loop(0, STEPS // 2, functools.partial(correct, (0, 2)), 0)
-    lax.fori_loop(0, STEPS // 4, functools.partial(correct_both, (0, 2)), 0)
+    lax.fori_loop(STEPS // 2, STEPS, functools.partial(correct, (0, 1, 2)), 0)
     begin_round(3)
-    lax.fori_loop(STEPS // 4, STEPS // 2, functools.partial(correct_both, (0, 1, 2)), 0)
+    lax.fori_loop(0, STEPS // 2, functools.partial(correct_strips, (0, 2)), 0)
+    lax.fori_loop(STEPS // 2, STEPS, functools.partial(correct_strips, (0, 1, 2)), 0)
 
     for k in range(4, len(rounds)):
         begin_round(k)
@@ -602,8 +595,7 @@
 
     lax.fori_loop(0, total // at_once, project, 0)
 
-    outs = []
-    for f, (field, strip, more, strip_more, out) in enumerate(((ef, se, ce, de, e_out), (hf, sh, ch, dh, h_out))):
+    for field, strip, more, strip_more, out in ((ef, se, ce, de, e_out), (hf, sh, ch, dh, h_out)):
         for c in range(3):
             for z in range(NZ):
                 half, j = z // HALF, z % HALF
@@ -612,10 +604,7 @@
                     value = field[c, z, at(g), :] + more[c, z, at(g, GHOST), :]
                     value = jnp.where(lane < 8, pltpu.roll(end, (CY - 64 * half - 8) % CY, 1), value)
                     value = jnp.where(lane >= CY - 8, pltpu.roll(end, 80 - 64 * half, 1), value)
-                    field[c, z, at(g), :] = value
-        copy = pltpu.make_async_copy(field.at[:, :, own_rows], out, out_sem.at[f])
-        copy.start()
-        outs.append(copy)
+                    out[c, z, pl.ds(8 * g, 8), :] = value
 
     pltpu.make_async_copy(f_recv, f_recv, f_recv_sem).wait()
     if total <= 64:
@@ -639,7 +628,16 @@
         return carry
 
     lax.fori_loop(0, STEPS, sent, 0)
-    for copy in outs:
+
+
+def write_out(e, h, far, e_out, h_out, far_out, sem):
+    copies = [
+        pltpu.make_async_copy(src, dst, sem.at[i])
+        for i, (src, dst) in enumerate(((e, e_out), (h, h_out), (far, far_out)))
+    ]
+    for copy in copies:
+        copy.start()
+    for copy in copies:
         copy.wait()
 
 
@@ -655,12 +653,12 @@
     e_out, h_out, far = pl.pallas_call(
         functools.partial(kernel, ny, nx, scale, starts),
         out_shape=(
-            jax.ShapeDtypeStruct(electric.shape, f32),
-            jax.ShapeDtypeStruct(electric.shape, f32),
-            jax.ShapeDtypeStruct((8, CY), f32),
+            pltpu.VMEM(electric.shape, f32),
+            pltpu.VMEM(electric.shape, f32),
+            pltpu.VMEM((8, CY), f32),
         ),
         in_specs=[hbm] * 8,
-        out_specs=(hbm, hbm, vmem),
+        out_specs=(vmem,) * 3,
         scratch_shapes=[
             pltpu.VMEM((3, NZ, PITCH, CY), f32),
             pltpu.VMEM((3, NZ, PITCH, CY), f32),
@@ -706,7 +704,6 @@
             pltpu.SemaphoreType.REGULAR((len(round_offsets(ny, nx)),)),
             pltpu.SemaphoreType.DMA,
             pltpu.SemaphoreType.DMA,
-            pltpu.SemaphoreType.DMA((2,)),
         ],
         compiler_params=pltpu.CompilerParams(
             collective_id=0, has_side_effects=True, vmem_limit_bytes=62 * 1024 * 1024
@@ -722,6 +719,14 @@
         band_table,
         packed,
     )
+    e_out, h_out, far = pl.pallas_call(
+        write_out,
+        out_shape=tuple(jax.ShapeDtypeStruct(value.shape, f32) for value in (e_out, h_out, far)),
+        in_specs=[vmem] * 3,
+        out_specs=(hbm,) * 3,
+        scratch_shapes=[pltpu.SemaphoreType.DMA((3,))],
+        name="write_out",
+    )(e_out, h_out, far)
     return e_out, h_out, far.reshape(1, 8, CY)
 
 

time: 34 us -> 31 us (0.912)
  Pallas kernels: 30 us -> 28.1 us
  local copies, waits for them, and re-layouts: 3.16 us -> 2.09 us
    pallas_call x1, Pallas kernels: 30 us -> 26.1 us  [local(): pl.pallas_call(functools.partial(kernel, ny, nx, scale, starts), out_shap...]
    pallas_call x0 -> x1, Pallas kernels: none -> 2.02 us  [local(): pl.pallas_call(write_out, out_shape=tuple((jax.ShapeDtypeStruct(value.sha...]
    unnamed x7 -> x6, local copies, waits for them, and re-layouts: 3.16 us -> 2.09 us
where the time goes in v4:
time: 31 us; the launch traced here: 30.9 us
  Pallas kernels  28.1 us (91%)
  local copies, waits for them, and re-layouts  2.09 us (7%)
  between operations  0.65 us (2%)
    pallas_call x1, Pallas kernels, local(): pl.pallas_call(functools.partial(kernel, ny, nx, scale, starts), out_shap...  26.1 us
    unnamed x6, local copies, waits for them, and re-layouts  2.09 us
    pallas_call x1, Pallas kernels, local(): pl.pallas_call(write_out, out_shape=tuple((jax.ShapeDtypeStruct(value.sha...  2.02 us

profile of v4, /device:TPU:0, one launch (start us, length us, event | category | flops | bytes accessed | tf_op | source)
XLA Modules:
  0.0 30.9 jit_solution(12885534121211719901)
XLA Ops:
  0.6 26.1 %fdtd.1 = (f32[3,16,16,128]{3,2,1,0:T(8,128)S(1)}, f32[3,16,16,128]{3,2,1,0:T(8,128)S(1)}, f32[8,128]{1,0:T(8,128)S(1)}) custom-call(f32[3,16,16,128]{3,2,1,0:T(8,128)} %e_hbm.1, f32[3,16,16,128]{3,2,1,0:T(8,128)} %h_hbm.1, s32[16,16,128]{2,1,0:T(8,128)} %ids_hbm.1, f32[8]{0:T(128)} %ca_hbm.1, f32[8]{0:T(128)} %cb_hbm.1, s32[4]{0:T(128)} %bitcast.2, ...), custom_call_target="tpu_custom_call" | custom-call | tf_op jit(solution)/shard_map/fdtd/pallas_call | solution.py:653
  26.8 0.0 copy-start
  26.8 0.7 %copy-done = f32[3,16,16,128]{3,2,1,0:T(8,128)} copy-done((f32[3,16,16,128]{3,2,1,0:T(8,128)}, f32[3,16,16,128]{3,2,1,0:T(8,128)S(1)}, u32[]{:S(2)}) %copy-start) | copy-done | bytes 393240
  27.5 0.0 copy-start.1
  27.5 0.8 %copy-done.1 = f32[3,16,16,128]{3,2,1,0:T(8,128)} copy-done((f32[3,16,16,128]{3,2,1,0:T(8,128)}, f32[3,16,16,128]{3,2,1,0:T(8,128)S(1)}, u32[]{:S(2)}) %copy-start.1) | copy-done | bytes 393240
  28.3 0.0 copy-start.2
  28.3 0.6 %copy-done.2 = f32[8,128]{1,0:T(8,128)} copy-done((f32[8,128]{1,0:T(8,128)}, f32[8,128]{1,0:T(8,128)S(1)}, u32[]{:S(2)}) %copy-start.2) | copy-done | bytes 4120
  28.9 2.0 %write_out.1 = (f32[3,16,16,128]{3,2,1,0:T(8,128)}, f32[3,16,16,128]{3,2,1,0:T(8,128)}, f32[8,128]{1,0:T(8,128)}) custom-call(f32[3,16,16,128]{3,2,1,0:T(8,128)} %copy-done, f32[3,16,16,128]{3,2,1,0:T(8,128)} %copy-done.1, f32[8,128]{1,0:T(8,128)} %copy-done.2), custom_call_target="tpu_custom_call" | custom-call | tf_op jit(solution)/shard_map/write_out/pallas_call | solution.py:722
Async XLA Ops:
  26.8 0.7 %copy-start = (f32[3,16,16,128]{3,2,1,0:T(8,128)}, f32[3,16,16,128]{3,2,1,0:T(8,128)S(1)}, u32[]{:S(2)}) copy-start(f32[3,16,16,128]{3,2,1,0:T(8,128)S(1)} %get-tuple-element.9.e) | copy-start | bytes 1179652
  27.5 0.8 %copy-start.1 = (f32[3,16,16,128]{3,2,1,0:T(8,128)}, f32[3,16,16,128]{3,2,1,0:T(8,128)S(1)}, u32[]{:S(2)}) copy-start(f32[3,16,16,128]{3,2,1,0:T(8,128)S(1)} %get-tuple-element.10.h) | copy-start | bytes 1179652
  28.3 0.6 %copy-start.2 = (f32[8,128]{1,0:T(8,128)}, f32[8,128]{1,0:T(8,128)S(1)}, u32[]{:S(2)}) copy-start(f32[8,128]{1,0:T(8,128)S(1)} %get-tuple-element.11.far) | copy-start | bytes 12292

commit v5 on v4

--- a/solution.py
+++ b/solution.py
@@ -726,7 +726,7 @@
         out_specs=(hbm,) * 3,
         scratch_shapes=[pltpu.SemaphoreType.DMA((3,))],
         name="write_out",
-    )(e_out, h_out, far)
+    )(*(pltpu.with_memory_space_constraint(value, pltpu.VMEM) for value in (e_out, h_out, far)))
     return e_out, h_out, far.reshape(1, 8, CY)
 
 

time: 31 us -> 27.8 us (0.90)
  local copies, waits for them, and re-layouts: 2.09 us -> 0 us
  Pallas kernels: 28.1 us -> 27 us
    unnamed x6 -> x0, local copies, waits for them, and re-layouts: 2.09 us -> none
    pallas_call x1, Pallas kernels: 2.02 us -> 0.91 us  [local(): pl.pallas_call(write_out, out_shape=tuple((jax.ShapeDtypeStruct(value.sha...]
where the time goes in v5:
time: 27.8 us; the launch traced here: 27.7 us
  Pallas kernels  27 us (97%)
  between operations  0.64 us (2%)
    pallas_call x1, Pallas kernels, local(): pl.pallas_call(functools.partial(kernel, ny, nx, scale, starts), out_shap...  26.1 us
    pallas_call x1, Pallas kernels, local(): pl.pallas_call(write_out, out_shape=tuple((jax.ShapeDtypeStruct(value.sha...  0.91 us

profile of v5, /device:TPU:0, one launch (start us, length us, event | category | flops | bytes accessed | tf_op | source)
XLA Modules:
  0.0 27.7 jit_solution(16368828422015739322)
XLA Ops:
  0.6 26.1 %fdtd.1 = (f32[3,16,16,128]{3,2,1,0:T(8,128)S(1)}, f32[3,16,16,128]{3,2,1,0:T(8,128)S(1)}, f32[8,128]{1,0:T(8,128)S(1)}) custom-call(f32[3,16,16,128]{3,2,1,0:T(8,128)} %e_hbm.1, f32[3,16,16,128]{3,2,1,0:T(8,128)} %h_hbm.1, s32[16,16,128]{2,1,0:T(8,128)} %ids_hbm.1, f32[8]{0:T(128)} %ca_hbm.1, f32[8]{0:T(128)} %cb_hbm.1, s32[4]{0:T(128)} %bitcast.2, ...), custom_call_target="tpu_custom_call" | custom-call | tf_op jit(solution)/shard_map/fdtd/pallas_call | solution.py:653
  26.8 0.9 %write_out.1 = (f32[3,16,16,128]{3,2,1,0:T(8,128)}, f32[3,16,16,128]{3,2,1,0:T(8,128)}, f32[8,128]{1,0:T(8,128)}) custom-call(f32[3,16,16,128]{3,2,1,0:T(8,128)S(1)} %get-tuple-element.9.e, f32[3,16,16,128]{3,2,1,0:T(8,128)S(1)} %get-tuple-element.10.h, f32[8,128]{1,0:T(8,128)S(1)} %get-tuple-element.11.far), custom_call_target="tpu_custom_call" | custom-call | tf_op jit(solution)/shard_map/write_out/pallas_call | solution.py:722

commit v6 on v5

--- a/solution.py
+++ b/solution.py
@@ -21,6 +21,7 @@
 HALO = 8
 ROWS = CX + 2 * HALO
 GHOST = 4
+EARLY = 2
 PITCH = CX + 2 * PAD
 WIDE = CX + 2 * GHOST + 2 * PAD
 OWN = (1, 2)
@@ -78,6 +79,7 @@
     coef_a, coef_b, se, sh, strip_a, strip_b, ce, ch, de, dh,
     edge_r, edge_l, from_l, from_r, last_ids, first_ids, left_ids, right_ids,
     own_h, own_e, left_h, right_e, strip_own_h, strip_own_e, strip_left_h, strip_right_e,
+    late_own_h, late_own_e, late_left_h, late_right_e,
     samples, strip_samples, sample, turned, acc, cols, phase, f_send, f_recv,
     send_sem, recv_sem, trace_send, trace_recv, round_sem, f_send_sem, f_recv_sem,
 ):
@@ -156,15 +158,17 @@
         (has_xl, has_xr, own_e, right_e, (iy, ix - 1)),
         (has_xr, has_xl, strip_own_h, strip_left_h, (iy, ix + 1)),
         (has_xl, has_xr, strip_own_e, strip_right_e, (iy, ix - 1)),
+        (has_xr, has_xl, late_own_h, late_left_h, (iy, ix + 1)),
+        (has_xl, has_xr, late_own_e, late_right_e, (iy, ix - 1)),
     )
 
     def trace(n, k):
         _, _, src, dst, device = traces[k]
         return pltpu.make_async_remote_copy(
-            src_ref=src.at[n],
-            dst_ref=dst.at[n],
-            send_sem=trace_send.at[n, k],
-            recv_sem=trace_recv.at[n, k],
+            src_ref=src.at[n - STEPS // 2 if k >= 4 else n],
+            dst_ref=dst.at[n - STEPS // 2 if k >= 4 else n],
+            send_sem=trace_send.at[n, 2 + k % 2 if k >= 4 else k],
+            recv_sem=trace_recv.at[n, 2 + k % 2 if k >= 4 else k],
             device_id=device,
             device_id_type=MESH,
         )
@@ -207,7 +211,10 @@
 
     y_copies, corner_copies, x_copies = range(2), range(2, 6), range(6, 8)
 
-    for given, fresh, arrived in ((has_xl, left_ids, (left_h, strip_left_h)), (has_xr, right_ids, (right_e, strip_right_e))):
+    for given, fresh, arrived in (
+        (has_xl, left_ids, (left_h, strip_left_h, late_left_h)),
+        (has_xr, right_ids, (right_e, strip_right_e, late_right_e)),
+    ):
         @pl.when(jnp.logical_not(given))
         def _(fresh=fresh, arrived=arrived):
             for buf in arrived:
@@ -240,27 +247,28 @@
     for load in loads:
         load.wait()
 
+    def pack_edges(which):
+        for i in which:
+            for g in range(2):
+                right = jnp.zeros((8, CY), f32)
+                left = jnp.zeros((8, CY), f32)
+                for z in range(NZ):
+                    if i < 6:
+                        value = (e_in, h_in)[i // 3][i % 3, z, pl.ds(8 * g, 8), :]
+                    else:
+                        value = ids[z, pl.ds(8 * g + HALO, 8), :].astype(f32)
+                    here = (lane >= 8 * z) & (lane < 8 * z + 8)
+                    right = jnp.where(here, pltpu.roll(value, (8 * z - 120) % CY, 1) if z < 15 else value, right)
+                    left = jnp.where(here, pltpu.roll(value, 8 * z, 1) if z else value, left)
+                edge_r[i, pl.ds(8 * g, 8), :] = right
+                edge_l[i, pl.ds(8 * g, 8), :] = left
+
     for z in range(NZ):
         spot = pl.ds(z * GHOST, GHOST)
         last_ids[spot, :] = ids[z, pl.ds(HALO + CX - GHOST, GHOST), :]
         first_ids[spot, :] = ids[z, pl.ds(HALO, GHOST), :]
     start_copies(x_copies)
-    for i in range(7):
-        for g in range(2):
-            right = jnp.zeros((8, CY), f32)
-            left = jnp.zeros((8, CY), f32)
-            for z in range(NZ):
-                rows = pl.ds(8 * g + PAD, 8)
-                if i < 6:
-                    value = (ef, hf)[i // 3][i % 3, z, rows, :]
-                else:
-                    value = ids[z, pl.ds(8 * g + HALO, 8), :].astype(f32)
-                here = (lane >= 8 * z) & (lane < 8 * z + 8)
-                right = jnp.where(here, pltpu.roll(value, (8 * z - 120) % CY, 1) if z < 15 else value, right)
-                left = jnp.where(here, pltpu.roll(value, 8 * z, 1) if z else value, left)
-            edge_r[i, pl.ds(8 * g, 8), :] = right
-            edge_l[i, pl.ds(8 * g, 8), :] = left
-    start_copies(y_copies)
+    pack_edges((6,))
     start_copies(corner_copies)
 
     def lookup(here):
@@ -326,19 +334,6 @@
         )
 
     coefficients(OWN)
-    rows_at_once = 8
-    for start in range(0, total, rows_at_once):
-        part = pl.ds(start, rows_at_once)
-        carry = (
-            jnp.full((rows_at_once, CY), scale, jnp.float32),
-            jnp.zeros((rows_at_once, CY), jnp.float32),
-            block.at(0, start, rows_at_once),
-            block.at(1, start, rows_at_once),
-        )
-        for bit in range(max(1, (nx - 1).bit_length())):
-            carry = power(bit, carry)
-        phase[part, :] = carry[0]
-        phase[pl.ds(total + start, rows_at_once), :] = carry[1]
     start_phase = Rows(phase, (0, total))
 
     half_y = jnp.where((in_half < 8) & (iy == 0), 0.0, 0.5).astype(f32)
@@ -430,15 +425,18 @@
         below = {g: tuple(jnp.where(low_half, 0.0, pltpu.roll(v, CY // 2, 1)) for v in below[g]) for g in groups}
         new_electric(e, h, strip_a, strip_b, 0, groups, base, plane(e, 0, groups), start, below, source_h)
 
-    def borders(n, e, h, mine_e, mine_h, run, k):
-        depth = e.shape[1]
+    def border(n, field, x, mine, late, k):
+        depth = field.shape[1]
         for c in (1, 2):
-            mine_e[n, pl.ds((c - 1) * depth, depth), :] = e[c, :, PAD, :]
-        send_trace(n, k + 1)
-        run(e, h, (0, 1), HALO)
-        for c in (1, 2):
-            mine_h[n, pl.ds((c - 1) * depth, depth), :] = h[c, :, PAD + CX - 1, :]
-        send_trace(n, k)
+            mine[n, pl.ds((c - 1) * depth, depth), :] = field[c, :, PAD + x, :]
+        if late is not None:
+            first, second = (mine[n, pl.ds(c * depth, depth), :] for c in range(2))
+            late[n - STEPS // 2] = jnp.where(in_middle, first, pltpu.roll(second, 16, 1))
+        if k < 2:
+            send_trace(n, k)
+
+    in_strip = lax.rem(lane, CY // 4)
+    in_middle = (in_strip >= 4) & (in_strip < 20)
 
     def keep(n, e, h, z, kept, first_row, add):
         for c, (field, part) in enumerate(((e, 0), (e, 1), (h, 0), (h, 1))):
@@ -448,12 +446,17 @@
                 kept[n, spot, :] = kept[n, spot, :] + value if add else value
 
     def alone(n, carry):
-        borders(n, ef, hf, own_e, own_h, advance, 0)
+        border(n, ef, 0, own_e, None, 1)
+        advance(ef, hf, (0, 1), HALO)
+        border(n, hf, CX - 1, own_h, None, 0)
         keep(n, ef, hf, ZF, samples, PAD, False)
         return carry
 
-    def alone_strips(n, carry):
-        borders(n, se, sh, strip_own_e, strip_own_h, advance_strips, 2)
+    def alone_strips(is_late, n, carry):
+        k = 4 if is_late else 2
+        border(n, se, 0, strip_own_e, late_own_e if is_late else None, k + 1)
+        advance_strips(se, sh, (0, 1), HALO)
+        border(n, sh, CX - 1, strip_own_h, late_own_h if is_late else None, k)
         keep(n, se, sh, 0, strip_samples, PAD, False)
         return carry
 
@@ -480,9 +483,15 @@
         keep(n, ce, ch, ZF, samples, PAD + GHOST, True)
         return carry
 
-    def correct_strips(groups, n, carry):
-        await_trace(n, 2)
-        await_trace(n, 3)
+    def correct_strips(groups, is_late, n, carry):
+        k = 4 if is_late else 2
+        await_trace(n, k)
+        await_trace(n, k + 1)
+        if is_late:
+            for late, buf in ((late_left_h, strip_left_h), (late_right_e, strip_right_e)):
+                both = late[n - STEPS // 2]
+                buf[n, pl.ds(0, HALF), :] = both
+                buf[n, pl.ds(HALF, HALF), :] = pltpu.roll(both, CY - 16, 1)
         advance_strips(
             de, dh, groups, SHIFT,
             sources(n, strip_own_e, strip_right_e, GHOST - 1, HALF), sources(n, strip_left_h, strip_own_h, GHOST, HALF),
@@ -490,12 +499,29 @@
         keep(n, de, dh, 0, strip_samples, PAD + GHOST, True)
         return carry
 
-    lax.fori_loop(0, STEPS, alone, 0)
+    lax.fori_loop(0, EARLY, alone, 0)
+    pack_edges(range(6))
+    start_copies(y_copies)
+    lax.fori_loop(EARLY, STEPS, alone, 0)
     begin_round(1)
     await_copies(y_copies)
     strips(OWN)
-    lax.fori_loop(0, STEPS, alone_strips, 0)
+    lax.fori_loop(0, STEPS // 2, functools.partial(alone_strips, False), 0)
+    lax.fori_loop(STEPS // 2, STEPS, functools.partial(alone_strips, True), 0)
     begin_round(2)
+    rows_at_once = 8
+    for start in range(0, total, rows_at_once):
+        part = pl.ds(start, rows_at_once)
+        carry = (
+            jnp.full((rows_at_once, CY), scale, jnp.float32),
+            jnp.zeros((rows_at_once, CY), jnp.float32),
+            block.at(0, start, rows_at_once),
+            block.at(1, start, rows_at_once),
+        )
+        for bit in range(max(1, (nx - 1).bit_length())):
+            carry = power(bit, carry)
+        phase[part, :] = carry[0]
+        phase[pl.ds(total + start, rows_at_once), :] = carry[1]
     await_copies(x_copies)
     await_copies(corner_copies)
     for z in range(NZ):
@@ -504,11 +530,19 @@
         ids[z, pl.ds(HALO + CX, GHOST), :] = right_ids[spot, :]
     strips((0, 3))
     coefficients((0, 3))
+
+    def send_strips(kinds, n, carry):
+        for k in kinds:
+            send_trace(n, k)
+        return carry
+
+    lax.fori_loop(0, STEPS // 2, functools.partial(send_strips, (2, 3)), 0)
+    lax.fori_loop(STEPS // 2, STEPS, functools.partial(send_strips, (4, 5)), 0)
     lax.fori_loop(0, STEPS // 2, functools.partial(correct, (0, 2)), 0)
     lax.fori_loop(STEPS // 2, STEPS, functools.partial(correct, (0, 1, 2)), 0)
     begin_round(3)
-    lax.fori_loop(0, STEPS // 2, functools.partial(correct_strips, (0, 2)), 0)
-    lax.fori_loop(STEPS // 2, STEPS, functools.partial(correct_strips, (0, 1, 2)), 0)
+    lax.fori_loop(0, STEPS // 2, functools.partial(correct_strips, (0, 2), False), 0)
+    lax.fori_loop(STEPS // 2, STEPS, functools.partial(correct_strips, (0, 1, 2), True), 0)
 
     for k in range(4, len(rounds)):
         begin_round(k)
@@ -620,14 +654,15 @@
         def _(i=i, src=src, dst=dst, device=device):
             remote(i, src, dst, device).wait_send()
 
-    def sent(n, carry):
-        for k in range(4):
+    def sent(kinds, n, carry):
+        for k in kinds:
             @pl.when(traces[k][0])
             def _(k=k):
                 trace(n, k).wait_send()
         return carry
 
-    lax.fori_loop(0, STEPS, sent, 0)
+    lax.fori_loop(0, STEPS // 2, functools.partial(sent, (0, 1, 2, 3)), 0)
+    lax.fori_loop(STEPS // 2, STEPS, functools.partial(sent, (0, 1, 4, 5)), 0)
 
 
 def write_out(e, h, far, e_out, h_out, far_out, sem):
@@ -688,6 +723,7 @@
             *[pltpu.VMEM((NZ * GHOST, CY), jnp.int32)] * 4,
             *[pltpu.VMEM((STEPS, 2 * NZ, CY), f32)] * 4,
             *[pltpu.VMEM((STEPS, 2 * HALF, CY), f32)] * 4,
+            *[pltpu.VMEM((STEPS // 2, HALF, CY), f32)] * 4,
             pltpu.VMEM((STEPS, 4 * CX, CY), f32),
             pltpu.VMEM((STEPS, 4 * CX, CY), f32),
             pltpu.VMEM((STEPS * 4 * CX, CY), f32),

time: 27.8 us -> 26.9 us (0.968)
  Pallas kernels: 27 us -> 26.1 us
    pallas_call x1, Pallas kernels: 26.1 us -> 25.2 us  [local(): pl.pallas_call(functools.partial(kernel, ny, nx, scale, starts), out_shap...]
where the time goes in v6:
time: 26.9 us; the launch traced here: 26.8 us
  Pallas kernels  26.1 us (97%)
  between operations  0.64 us (2%)
    pallas_call x1, Pallas kernels, local(): pl.pallas_call(functools.partial(kernel, ny, nx, scale, starts), out_shap...  25.2 us
    pallas_call x1, Pallas kernels, local(): pl.pallas_call(write_out, out_shape=tuple((jax.ShapeDtypeStruct(value.sha...  0.91 us

profile of v6, /device:TPU:0, one launch (start us, length us, event | category | flops | bytes accessed | tf_op | source)
XLA Modules:
  0.0 26.8 jit_solution(17947974109150760308)
XLA Ops:
  0.6 25.2 %fdtd.1 = (f32[3,16,16,128]{3,2,1,0:T(8,128)S(1)}, f32[3,16,16,128]{3,2,1,0:T(8,128)S(1)}, f32[8,128]{1,0:T(8,128)S(1)}) custom-call(f32[3,16,16,128]{3,2,1,0:T(8,128)} %e_hbm.1, f32[3,16,16,128]{3,2,1,0:T(8,128)} %h_hbm.1, s32[16,16,128]{2,1,0:T(8,128)} %ids_hbm.1, f32[8]{0:T(128)} %ca_hbm.1, f32[8]{0:T(128)} %cb_hbm.1, s32[4]{0:T(128)} %bitcast.2, ...), custom_call_target="tpu_custom_call" | custom-call | tf_op jit(solution)/shard_map/fdtd/pallas_call | solution.py:688
  25.9 0.9 %write_out.1 = (f32[3,16,16,128]{3,2,1,0:T(8,128)}, f32[3,16,16,128]{3,2,1,0:T(8,128)}, f32[8,128]{1,0:T(8,128)}) custom-call(f32[3,16,16,128]{3,2,1,0:T(8,128)S(1)} %get-tuple-element.9.e, f32[3,16,16,128]{3,2,1,0:T(8,128)S(1)} %get-tuple-element.10.h, f32[8,128]{1,0:T(8,128)S(1)} %get-tuple-element.11.far), custom_call_target="tpu_custom_call" | custom-call | tf_op jit(solution)/shard_map/write_out/pallas_call | solution.py:758

commit v7 on v6

--- a/solution.py
+++ b/solution.py
@@ -109,8 +109,6 @@
             )
         )
     ]
-    for load in loads:
-        load.start()
     time, y_start, cell, block = (Rows(table, starts[i : i + 2]) for i in (2, 4, 6, 8))
 
     barrier = pltpu.get_barrier_semaphore()
@@ -132,6 +130,8 @@
 
     around = [(dy, dx) for dy in (-1, 0, 1) for dx in (-1, 0, 1) if (dy, dx) != (0, 0)]
     signal_all(barrier, around)
+    for load in loads:
+        load.start()
     rounds = round_offsets(ny, nx)
 
     def begin_round(k):
@@ -640,6 +640,22 @@
                     value = jnp.where(lane >= CY - 8, pltpu.roll(end, 80 - 64 * half, 1), value)
                     out[c, z, pl.ds(8 * g, 8), :] = value
 
+    for i, (sends, _, src, dst, device) in enumerate(every):
+        @pl.when(sends)
+        def _(i=i, src=src, dst=dst, device=device):
+            remote(i, src, dst, device).wait_send()
+
+    def sent(kinds, n, carry):
+        for k in kinds:
+            @pl.when(traces[k][0])
+            def _(k=k):
+                trace(n, k).wait_send()
+        return carry
+
+    lax.fori_loop(0, STEPS // 2, functools.partial(sent, (0, 1, 2, 3)), 0)
+    lax.fori_loop(STEPS // 2, STEPS, functools.partial(sent, (0, 1, 4, 5)), 0)
+    pltpu.make_async_copy(f_recv, f_recv, f_send_sem).wait()
+
     pltpu.make_async_copy(f_recv, f_recv, f_recv_sem).wait()
     if total <= 64:
         terms = [f_send[0]] + [f_recv[k] for k in range(total - 1)]
@@ -648,21 +664,6 @@
         far_out[...] = terms[0]
     else:
         far_out[...] = lax.fori_loop(0, total - 1, lambda k, t: t + f_recv[k], f_send[0])
-    pltpu.make_async_copy(f_recv, f_recv, f_send_sem).wait()
-    for i, (sends, _, src, dst, device) in enumerate(every):
-        @pl.when(sends)
-        def _(i=i, src=src, dst=dst, device=device):
-            remote(i, src, dst, device).wait_send()
-
-    def sent(kinds, n, carry):
-        for k in kinds:
-            @pl.when(traces[k][0])
-            def _(k=k):
-                trace(n, k).wait_send()
-        return carry
-
-    lax.fori_loop(0, STEPS // 2, functools.partial(sent, (0, 1, 2, 3)), 0)
-    lax.fori_loop(STEPS // 2, STEPS, functools.partial(sent, (0, 1, 4, 5)), 0)
 
 
 def write_out(e, h, far, e_out, h_out, far_out, sem):

time: 26.9 us -> 26.8 us (level)
  no operation moved by 1% of the time
where the time goes in v7:
time: 26.8 us; the launch traced here: 26.7 us
  Pallas kernels  26 us (97%)
  between operations  0.64 us (2%)
    pallas_call x1, Pallas kernels, local(): pl.pallas_call(functools.partial(kernel, ny, nx, scale, starts), out_shap...  25.1 us
    pallas_call x1, Pallas kernels, local(): pl.pallas_call(write_out, out_shape=tuple((jax.ShapeDtypeStruct(value.sha...  0.91 us

profile of v7, /device:TPU:0, one launch (start us, length us, event | category | flops | bytes accessed | tf_op | source)
XLA Modules:
  0.0 26.7 jit_solution(9859389815835319038)
XLA Ops:
  0.6 25.1 %fdtd.1 = (f32[3,16,16,128]{3,2,1,0:T(8,128)S(1)}, f32[3,16,16,128]{3,2,1,0:T(8,128)S(1)}, f32[8,128]{1,0:T(8,128)S(1)}) custom-call(f32[3,16,16,128]{3,2,1,0:T(8,128)} %e_hbm.1, f32[3,16,16,128]{3,2,1,0:T(8,128)} %h_hbm.1, s32[16,16,128]{2,1,0:T(8,128)} %ids_hbm.1, f32[8]{0:T(128)} %ca_hbm.1, f32[8]{0:T(128)} %cb_hbm.1, s32[4]{0:T(128)} %bitcast.2, ...), custom_call_target="tpu_custom_call" | custom-call | tf_op jit(solution)/shard_map/fdtd/pallas_call | solution.py:689
  25.8 0.9 %write_out.1 = (f32[3,16,16,128]{3,2,1,0:T(8,128)}, f32[3,16,16,128]{3,2,1,0:T(8,128)}, f32[8,128]{1,0:T(8,128)}) custom-call(f32[3,16,16,128]{3,2,1,0:T(8,128)S(1)} %get-tuple-element.9.e, f32[3,16,16,128]{3,2,1,0:T(8,128)S(1)} %get-tuple-element.10.h, f32[8,128]{1,0:T(8,128)S(1)} %get-tuple-element.11.far), custom_call_target="tpu_custom_call" | custom-call | tf_op jit(solution)/shard_map/write_out/pallas_call | solution.py:759
